TPU v7x, 256 devices: a whole 4x4x8 slice. The times are simulated.
256 devices in a mesh: region: 2 (over z_lo), ax: 8 (over x, core), az: 16 (over z_hi, y).
Axes of the slice: x: 4, y: 4, z: 8 (z_hi: 4, z_lo: 2; z = z_hi * 2 + z_lo), core: 2. Of those that a mesh axis runs over, the one named last changes fastest.
Arguments:
- state: float32 [2, 3, 128, 128, 2048], P('region', None, None, 'az', 'ax'), may hold values from -6 to 6
- conduct: float32 [2, 128, 128, 2048], P('region', None, 'az', 'ax'), may hold values from 0.25 to 2
- zones: int32 [2048], P('ax'), may hold values from 0 to 2, never falling along the last dimension, each value on 1 to 1024 neighbouring positions
- placement: int32 [2048], P('ax'), may hold values from 0 to 127
Outputs:
- new_state: float32 [2, 3, 128, 128, 2048], P('region', None, None, 'az', 'ax')
Inputs may be any that keep to these rules, and one draw needn't show every extreme that they name: `zones`: 0 evaporator, 1 adiabatic, 2 condenser, never falling along the axis; each zone has 1 to 1024 cells and one has exactly 1024.
All inputs are finite; a program needn't handle non-finite values.
Results may differ from a plain program's by a relative error of at most 0.00002.
Values sent between devices are 32-bit elements; how exact they have to be, the bound alone decides.
A program may use at most 64 MiB of HBM per device.

v0:
```python
import jax
import jax.numpy as jnp
from jax import lax
from jax.sharding import PartitionSpec as P

time_step = 0.05


def swapped(value, axis, bit):
    mask = 2**bit
    pairs = [(source, source ^ mask) for source in range(lax.axis_size(axis))]
    return lax.ppermute(value, axis, pairs)


def with_halo(cells, sides, width, closed):
    for axis, dim in sides:
        count = lax.axis_size(axis)
        ends = count if closed else count - 1
        head = lax.slice_in_dim(cells, 0, width, axis=dim)
        tail = lax.slice_in_dim(cells, cells.shape[dim] - width, cells.shape[dim], axis=dim)
        cells = jnp.concatenate(
            [
                lax.ppermute(tail, axis, [(i, (i + 1) % count) for i in range(ends)]),
                cells,
                lax.ppermute(head, axis, [((i + 1) % count, i) for i in range(ends)]),
            ],
            axis=dim,
        )
    return cells


def select_rows(source, wanted):
    count = source.shape[1]
    slots = jnp.arange(count, dtype=jnp.int32)[:, None, None]
    chosen = slots == wanted[None, :, :]
    picked = jnp.where(chosen[None], source[:, :, None, :], jnp.float32(0.0))
    return jnp.sum(picked, axis=1)


def rotate(strip, shift, az_cells):
    cycle_size = az_cells * lax.axis_size("az")
    width = strip.shape[2] // lax.axis_size("az")
    local_shift = lax.dynamic_slice_in_dim(shift, lax.axis_index("az") * width, width, 0)
    circle = jnp.arange(cycle_size, dtype=jnp.int32)
    turn_index = (circle[:, None] + local_shift[None, :]) % cycle_size
    turned = select_rows(
        lax.all_to_all(strip, "az", split_axis=2, concat_axis=1, tiled=True), turn_index
    )
    return lax.all_to_all(turned, "az", split_axis=1, concat_axis=2, tiled=True)


def on_device(state, conduct, zones, placement):
    fields = state[0]
    kappa = conduct[0]
    radial, az_cells = (fields.shape[1], fields.shape[2])
    is_vapor = lax.axis_index("region") == 0
    cycle_size = az_cells * lax.axis_size("az")
    own_layer = jnp.where(is_vapor, fields[:, radial - 1], fields[:, 0])
    own_sign = jnp.where(is_vapor, 1, -1).astype(jnp.int32)
    received = swapped(own_layer, "region", 0)
    partner = rotate(received, own_sign * placement % cycle_size, az_cells)
    az_pad = with_halo(fields, (("az", 2),), 1, True)
    ax_pad = with_halo(fields, (("ax", 3),), 1, False)
    t_wick = jnp.where(is_vapor, partner[0], own_layer[0])
    p_vapor = jnp.where(is_vapor, own_layer[1], partner[1])
    u_vapor = jnp.where(is_vapor, own_layer[2], partner[2])
    u_wick = jnp.where(is_vapor, partner[2], own_layer[2])
    evap = 2.0 * (t_wick - 0.5 * p_vapor)
    shear = 1.5 * (u_vapor - u_wick)
    layer_t = jnp.where(is_vapor, 0.5 * evap, -evap)
    layer_p = jnp.where(is_vapor, evap, -0.5 * evap)
    layer_u = jnp.where(is_vapor, -shear, 0.5 * shear)
    radii = jnp.arange(radial, dtype=jnp.int32)
    iface_row = jnp.where(is_vapor, radial - 1, 0)
    iface_mask = (radii == iface_row).astype(jnp.float32)[:, None, None]
    wall_mask = jnp.logical_and(radii == radial - 1, jnp.logical_not(is_vapor)).astype(jnp.float32)[
        :, None, None
    ]
    wall_temp = fields[0, radial - 1]
    wall_heat = jnp.where(
        zones[None, :] == 0,
        jnp.float32(2.0),
        jnp.where(zones[None, :] == 2, -1.5 * (wall_temp + 1.0), jnp.float32(0.0)),
    )
    src_t = iface_mask * layer_t[None] + wall_mask * wall_heat[None]
    src_p = iface_mask * layer_p[None]
    src_u = iface_mask * layer_u[None]
    outward = jnp.concatenate([fields[:, 1:], fields[:, -1:]], axis=1)
    inward = jnp.concatenate([fields[:, :1], fields[:, :-1]], axis=1)
    az_plus = az_pad[:, :, 2:]
    az_minus = az_pad[:, :, :-2]
    ax_plus = ax_pad[..., 2:]
    ax_minus = ax_pad[..., :-2]
    laplace = outward + inward + az_plus + az_minus + ax_plus + ax_minus - 6.0 * fields
    gradient = 0.5 * (ax_plus - ax_minus)
    press_coef = jnp.where(is_vapor, jnp.float32(1.0), jnp.float32(0.6))
    visc_coef = jnp.where(is_vapor, jnp.float32(0.3), jnp.float32(0.05))
    fric_coef = jnp.where(is_vapor, jnp.float32(0.1), jnp.float32(2.0))
    sound_coef = jnp.where(is_vapor, jnp.float32(1.5), jnp.float32(0.8))
    pdiff_coef = jnp.where(is_vapor, jnp.float32(0.2), jnp.float32(0.4))
    advect_coef = jnp.where(is_vapor, jnp.float32(1.0), jnp.float32(0.5))
    temper, press, veloc = (fields[0], fields[1], fields[2])
    new_t = temper + time_step * (kappa * laplace[0] - advect_coef * veloc * gradient[0] + src_t)
    new_p = press + time_step * (-sound_coef * gradient[2] + pdiff_coef * laplace[1] + src_p)
    new_u = veloc + time_step * (
        -press_coef * gradient[1] + visc_coef * laplace[2] - fric_coef * veloc + src_u
    )
    return jnp.stack([new_t, new_p, new_u])[None]


def solution(mesh):
    return jax.shard_map(
        on_device,
        mesh=mesh,
        in_specs=(
            P("region", None, None, "az", "ax"),
            P("region", None, "az", "ax"),
            P("ax"),
            P("ax"),
        ),
        out_specs=P("region", None, None, "az", "ax"),
        check_vma=False,
    )
```

profile of v0, /device:TPU:1, one launch (start us, length us, event | category | flops | bytes accessed | tf_op | source)
XLA Modules:
  0.0 82.3 jit_solution(1671787079106821845)
XLA Ops:
  0.8 2.5 %collective-permute-start.4 = (f32[3,8,256]{2,1,0:T(8,128)S(1)}, f32[3,8,256]{2,1,0:T(8,128)S(1)}, u32[]{:S(2)}, u32[]{:S(2)}) collective-permute-start(f32[3,8,256]{2,1,0:T(8,128)S(1)} %bitcast.79), channel_id=1, source_target_pairs={{0,128},{128,0},{1,129},{129,1},{2,130},{130,2},{3,131},{131,3},{4... | collective-permute-start | bytes 73736 | tf_op jit(solution)/shard_map/ppermute | solution.py:12
  3.2 4.0 %fusion.32 = (f32[3,128,8,1]{3,2,1,0:T(8,128)}, f32[3,128,8,1]{3,2,1,0:T(8,128)}) fusion(f32[3,128,8,256]{3,2,1,0:T(8,128)} %bitcast.68), kind=kLoop, calls=%fused_computation.67 | loop fusion | bytes 49152 | tf_op jit(solution)/shard_map/slice | solution.py:20
  7.3 2.0 %copy.20 = f32[3,128,8,1]{1,2,3,0:T(8,128)S(1)} copy(f32[3,128,8,1]{3,2,1,0:T(8,128)} %get-tuple-element.15) | data formatting | bytes 24576 | tf_op jit(solution)/shard_map/slice | solution.py:19
  9.3 2.9 %collective-permute-start.2 = (f32[3,128,8,1]{1,2,3,0:T(8,128)S(1)}, f32[3,128,8,1]{1,2,3,0:T(8,128)}, u32[]{:S(2)}, u32[]{:S(2)}) collective-permute-start(f32[3,128,8,1]{1,2,3,0:T(8,128)S(1)} %copy.20), channel_id=1, source_target_pairs={{16,0},{32,16},{48,32},{64,48},{80,64},{96,80},{112,96},{17,1},{33... | collective-permute-start | bytes 36872 | tf_op jit(solution)/shard_map/ppermute | solution.py:25
  12.2 2.5 %copy.22 = f32[3,128,8,1]{1,2,3,0:T(8,128)} copy(f32[3,128,8,1]{3,2,1,0:T(8,128)} %get-tuple-element.14) | data formatting | bytes 24576 | tf_op jit(solution)/shard_map/slice | solution.py:20
  14.7 3.0 %collective-permute-start.3 = (f32[3,128,8,1]{1,2,3,0:T(8,128)}, f32[3,128,8,1]{1,2,3,0:T(8,128)}, u32[]{:S(2)}, u32[]{:S(2)}) collective-permute-start(f32[3,128,8,1]{1,2,3,0:T(8,128)} %copy.22), channel_id=1, source_target_pairs={{0,16},{16,32},{32,48},{48,64},{64,80},{80,96},{96,112},{1,17},{17... | collective-permute-start | bytes 36872 | tf_op jit(solution)/shard_map/ppermute | solution.py:23
  17.7 1.4 %fusion.34 = (f32[3,128,1,256]{3,2,1,0:T(1,128)}, f32[3,128,1,256]{3,2,1,0:T(1,128)}) fusion(f32[3,128,8,256]{3,2,1,0:T(8,128)S(1)} %bitcast.69), kind=kLoop, calls=%fused_computation.69 | loop fusion | bytes 1572864 | tf_op jit(solution)/shard_map/slice | solution.py:19
  19.1 7.6 %collective-permute-start = (f32[3,128,1,256]{3,2,1,0:T(1,128)}, f32[3,128,1,256]{3,2,1,0:T(1,128)}, u32[]{:S(2)}, u32[]{:S(2)}) collective-permute-start(f32[3,128,1,256]{3,2,1,0:T(1,128)} %get-tuple-element.18), channel_id=1, source_target_pairs={{1,0},{2,1},{3,2},{4,3},{5,4},{6,5},{7,6},{8,7},{9,8},{10,9},{11,1... | collective-permute-start | bytes 1179656 | tf_op jit(solution)/shard_map/ppermute | solution.py:25
  26.6 3.2 %fusion.33 = (f32[3,127,8,256]{3,2,1,0:T(8,128)}, f32[3,127,8,256]{3,2,1,0:T(8,128)}) fusion(f32[3,128,8,256]{3,2,1,0:T(8,128)S(1)} %bitcast.70), kind=kLoop, calls=%fused_computation.68 | loop fusion | bytes 12484608 | tf_op jit(solution)/shard_map/slice | solution.py:89
  30.2 1.0 %copy.24 = f32[3,8,256]{1,0,2:T(4,128)} copy(f32[3,8,256]{2,1,0:T(8,128)S(1)} %collective-permute-done.4) | data formatting | bytes 49152 | tf_op jit(solution)/shard_map/ppermute | solution.py:12
  31.2 2.0 %reshape.151 = f32[16,1,384]{2,1,0:T(1,128)} reshape(f32[256,3,8]{2,1,0:T(4,128)} %bitcast.73) | data formatting | bytes 49152
  33.1 7.1 %all-to-all-start = ((f32[16,1,384]{2,1,0:T(1,128)}), f32[16,1,384]{2,1,0:T(1,128)S(1)}, u32[]{:S(2)}, u32[]{:S(2)}) async-start(f32[16,1,384]{2,1,0:T(1,128)} %reshape.151), calls=%async_computation | async-start | bytes 49152 | tf_op jit(solution)/shard_map/all_to_all | solution.py:47
  40.2 10.3 %all-to-all-done = f32[16,1,384]{2,1,0:T(1,128)S(1)} async-done(((f32[16,1,384]{2,1,0:T(1,128)}), f32[16,1,384]{2,1,0:T(1,128)S(1)}, u32[]{:S(2)}, u32[]{:S(2)}) %all-to-all-start) | async-done | bytes 24608 | tf_op jit(solution)/shard_map/all_to_all | solution.py:47
  51.7 1.1 %reshape.152 = f32[256,3,8]{2,1,0:T(4,128)} reshape(f32[16,384]{1,0:T(8,128)S(1)} %reduce) | data formatting | bytes 49152
  52.8 1.9 %copy.25 = f32[3,8,16,16]{3,1,2,0:T(8,128)} copy(f32[3,8,16,16]{1,0,3,2:T(4,128)} %bitcast.74) | data formatting | bytes 49152 | tf_op jit(solution)/shard_map/all_to_all | solution.py:47
  54.7 1.9 %select_reduce_fusion = f32[3,128,16]{1,2,0:T(8,128)S(1)} fusion(f32[3,128,16]{2,1,0:T(8,128)} %bitcast.78, pred[128,128,16]{1,2,0:T(8,128)(4,1)S(1)} %iota_compare_fusion), kind=kLoop, calls=%fused_computation.11 | loop fusion | flops 1566720 | bytes 311296 | tf_op jit(solution)/shard_map/reduce_sum | solution.py:37
  57.5 4.7 %all-to-all-start.1 = ((f32[16,1,384]{2,1,0:T(1,128)}), f32[16,1,384]{2,1,0:T(1,128)S(1)}, u32[]{:S(2)}, u32[]{:S(2)}) async-start(f32[16,1,384]{2,1,0:T(1,128)} %reshape.153), calls=%async_computation.1 | async-start | bytes 49152 | tf_op jit(solution)/shard_map/all_to_all | solution.py:49
  62.9 2.4 %copy.21 = f32[3,128,8,1]{3,2,1,0:T(8,128)} copy(f32[3,128,8,1]{1,2,3,0:T(8,128)} %collective-permute-done.2) | data formatting | bytes 24576 | tf_op jit(solution)/shard_map/ppermute | solution.py:25
  65.2 2.4 %copy.23 = f32[3,128,8,1]{3,2,1,0:T(8,128)} copy(f32[3,128,8,1]{1,2,3,0:T(8,128)} %collective-permute-done.3) | data formatting | bytes 24576 | tf_op jit(solution)/shard_map/ppermute | solution.py:23
  67.6 3.5 %all-to-all-done.1 = f32[16,1,384]{2,1,0:T(1,128)S(1)} async-done(((f32[16,1,384]{2,1,0:T(1,128)}), f32[16,1,384]{2,1,0:T(1,128)S(1)}, u32[]{:S(2)}, u32[]{:S(2)}) %all-to-all-start.1) | async-done | bytes 24608 | tf_op jit(solution)/shard_map/all_to_all | solution.py:49
  72.4 5.9 %subtract_multiply_fusion = (f32[3,128,8,256]{3,2,1,0:T(8,128)S(1)}, f32[3,128,8,256]{3,2,1,0:T(8,128)S(1)}) fusion(f32[3,128,8,1]{3,2,1,0:T(8,128)} %copy.21, f32[3,128,8,256]{3,2,1,0:T(8,128)S(1)} %bitcast.72, f32[3,128,8,1]{3,2,1,0:T(8,128)} %copy.23, f32[3,128,1,256]{3,2,1,0:T(1,128)} %collective-permute-done.1, ...), kind=kLoop, calls=%fused_computation.12 | loop fusion | flops 11796480 | bytes 16539648 | tf_op jit(solution)/shard_map/mul | solution.py:95
  78.6 0.9 %copy-done.1 = f32[1,128,8,256]{3,2,1,0:T(8,128)S(1)} copy-done((f32[1,128,8,256]{3,2,1,0:T(8,128)S(1)}, f32[1,128,8,256]{3,2,1,0:T(8,128)}, u32[]{:S(2)}) %copy-start.1) | copy-done | bytes 1048600
  79.5 0.9 %fusion.17 = (f32[1,128,8,256]{3,2,1,0:T(8,128)S(1)}, f32[1,128,8,256]{3,2,1,0:T(8,128)S(1)}) fusion(f32[3,128,8,256]{3,2,1,0:T(8,128)S(1)} %get-tuple-element.9, f32[1,128,8,256]{3,2,1,0:T(8,128)S(1)} %copy-done.1, f32[3,128,8,256]{3,2,1,0:T(8,128)S(1)} %get-tuple-element.10, f32[1,3,128,8,256]{4,3,2,1,0:T(8,128)S(1)} %copy-done, f32[8,256]{1,0:T(8,128)S(1)} %fusion.22, ...), kind=kLoop, calls=%fused_computation.30 | loop fusion | flops 4980736 | bytes 9462800 | tf_op jit(solution)/shard_map/add | solution.py:103
  80.4 1.9 %maximum_bitcast_fusion = f32[1,3,128,8,256]{4,3,2,1,0:T(8,128)} fusion(f32[1,128,8,256]{3,2,1,0:T(8,128)S(1)} %get-tuple-element.8, f32[1,128,8,256]{3,2,1,0:T(8,128)S(1)} %fusion.13, f32[1,128,8,256]{3,2,1,0:T(8,128)S(1)} %get-tuple-element.7), kind=kLoop, calls=%fused_computation.10 | loop fusion | flops 1572864 | bytes 6291456 | tf_op jit(solution)/shard_map/broadcast_in_dim | solution.py:108
  (40 shorter events, 5.2 us)
Async XLA Ops:
  0.8 29.4 %collective-permute-start.4 = (f32[3,8,256]{2,1,0:T(8,128)S(1)}, f32[3,8,256]{2,1,0:T(8,128)S(1)}, u32[]{:S(2)}, u32[]{:S(2)}) collective-permute-start(f32[3,8,256]{2,1,0:T(8,128)S(1)} %bitcast.79), channel_id=1, source_target_pairs={{0,128},{128,0},{1,129},{129,1},{2,130},{130,2},{3,131},{131,3},{4... | collective-permute-start | bytes 73736 | tf_op jit(solution)/shard_map/ppermute | solution.py:12
  7.3 10.4 %copy-start = (f32[1,3,128,8,256]{4,3,2,1,0:T(8,128)S(1)}, f32[1,3,128,8,256]{4,3,2,1,0:T(8,128)}, u32[]{:S(2)}) copy-start(f32[1,3,128,8,256]{4,3,2,1,0:T(8,128)} %param.4) | copy-start | bytes 9437188
  9.3 53.6 %collective-permute-start.2 = (f32[3,128,8,1]{1,2,3,0:T(8,128)S(1)}, f32[3,128,8,1]{1,2,3,0:T(8,128)}, u32[]{:S(2)}, u32[]{:S(2)}) collective-permute-start(f32[3,128,8,1]{1,2,3,0:T(8,128)S(1)} %copy.20), channel_id=1, source_target_pairs={{16,0},{32,16},{48,32},{64,48},{80,64},{96,80},{112,96},{17,1},{33... | collective-permute-start | bytes 36872 | tf_op jit(solution)/shard_map/ppermute | solution.py:25
  14.7 50.6 %collective-permute-start.3 = (f32[3,128,8,1]{1,2,3,0:T(8,128)}, f32[3,128,8,1]{1,2,3,0:T(8,128)}, u32[]{:S(2)}, u32[]{:S(2)}) collective-permute-start(f32[3,128,8,1]{1,2,3,0:T(8,128)} %copy.22), channel_id=1, source_target_pairs={{0,16},{16,32},{32,48},{48,64},{64,80},{80,96},{96,112},{1,17},{17... | collective-permute-start | bytes 36872 | tf_op jit(solution)/shard_map/ppermute | solution.py:23
  19.1 53.3 %collective-permute-start = (f32[3,128,1,256]{3,2,1,0:T(1,128)}, f32[3,128,1,256]{3,2,1,0:T(1,128)}, u32[]{:S(2)}, u32[]{:S(2)}) collective-permute-start(f32[3,128,1,256]{3,2,1,0:T(1,128)} %get-tuple-element.18), channel_id=1, source_target_pairs={{1,0},{2,1},{3,2},{4,3},{5,4},{6,5},{7,6},{8,7},{9,8},{10,9},{11,1... | collective-permute-start | bytes 1179656 | tf_op jit(solution)/shard_map/ppermute | solution.py:25
  26.6 3.2 %copy-start.3 = (s32[256]{0:T(256)S(1)}, s32[256]{0:T(256)}, u32[]{:S(2)}) copy-start(s32[256]{0:T(256)} %param.7) | copy-start | bytes 3076
  26.6 3.5 %copy-start.4 = (s32[256]{0:T(256)S(1)}, s32[256]{0:T(256)}, u32[]{:S(2)}) copy-start(s32[256]{0:T(256)} %param.6) | copy-start | bytes 3076
  26.6 45.8 %collective-permute-start.1 = (f32[3,128,1,256]{3,2,1,0:T(1,128)}, f32[3,128,1,256]{3,2,1,0:T(1,128)}, u32[]{:S(2)}, u32[]{:S(2)}) collective-permute-start(f32[3,128,1,256]{3,2,1,0:T(1,128)} %get-tuple-element.19), channel_id=1, source_target_pairs={{0,1},{1,2},{2,3},{3,4},{4,5},{5,6},{6,7},{7,8},{8,9},{9,10},{10,1... | collective-permute-start | bytes 1179656 | tf_op jit(solution)/shard_map/ppermute | solution.py:23
  33.1 17.4 %all-to-all-start = ((f32[16,1,384]{2,1,0:T(1,128)}), f32[16,1,384]{2,1,0:T(1,128)S(1)}, u32[]{:S(2)}, u32[]{:S(2)}) async-start(f32[16,1,384]{2,1,0:T(1,128)} %reshape.151), calls=%async_computation | async-start | bytes 49152 | tf_op jit(solution)/shard_map/all_to_all | solution.py:47
  57.5 13.6 %all-to-all-start.1 = ((f32[16,1,384]{2,1,0:T(1,128)}), f32[16,1,384]{2,1,0:T(1,128)S(1)}, u32[]{:S(2)}, u32[]{:S(2)}) async-start(f32[16,1,384]{2,1,0:T(1,128)} %reshape.153), calls=%async_computation.1 | async-start | bytes 49152 | tf_op jit(solution)/shard_map/all_to_all | solution.py:49
  78.3 1.2 %copy-start.1 = (f32[1,128,8,256]{3,2,1,0:T(8,128)S(1)}, f32[1,128,8,256]{3,2,1,0:T(8,128)}, u32[]{:S(2)}) copy-start(f32[1,128,8,256]{3,2,1,0:T(8,128)} %param.5) | copy-start | bytes 3145732
  78.3 1.2 %copy-start.2 = (f32[128]{0:T(128)S(1)}, f32[128]{0:T(128)}, u32[]{:S(2)}) copy-start(f32[128]{0:T(128)} %get-tuple-element.26) | copy-start | bytes 1540
where the time goes:
time: 83.6 us; the launch traced here: 82.3 us
  starting transfers between devices  27.7 us (33%)
  local copies, waits for them, and re-layouts  26.8 us (32%)
  waiting for transfers between devices  13.9 us (17%)
  other arithmetic  13.7 us (16%)
    ppermute x2, starting transfers between devices, with_halo(): lax.ppermute(head, axis, [((i + 1) % count, i) for i in range(ends)])  10.4 us
    all_to_all x1, waiting for transfers between devices, rotate(): lax.all_to_all(strip, 'az', split_axis=2, concat_axis=1, tiled=True)  10.3 us
    all_to_all x1, starting transfers between devices, rotate(): lax.all_to_all(strip, 'az', split_axis=2, concat_axis=1, tiled=True)  7.06 us
    slice x2, local copies, waits for them, and re-layouts, with_halo(): lax.slice_in_dim(cells, cells.shape[dim] - width, cells.shape[dim], axis=...  6.52 us
    mul x1, other arithmetic, on_device(): gradient = 0.5 * (ax_plus - ax_minus)  5.86 us
    unnamed x14, local copies, waits for them, and re-layouts  4.97 us
    all_to_all x1, starting transfers between devices, rotate(): return lax.all_to_all(turned, 'az', split_axis=1, concat_axis=2, tiled=True)  4.73 us
    all_to_all x1, waiting for transfers between devices, rotate(): return lax.all_to_all(turned, 'az', split_axis=1, concat_axis=2, tiled=True)  3.51 us
  transfers between devices with their start and end apart: 7, of which 2 were waited for; matrix products, arithmetic and copies ran while one was open for 36% of the time, Pallas kernels for 0%

commit v1 on v0

v1 whole, which is shorter than its diff:
```python
import functools
import jax
import jax.numpy as jnp
from jax import lax
from jax.experimental import pallas as pl
from jax.experimental.pallas import tpu as pltpu
from jax.sharding import PartitionSpec as P

MESH = pl.DeviceIdType.MESH
dt = 0.05
chunks = 8
unroll = 4


def step_kernel(
    state, conduct, zone_ref, place_ref, out,
    zones, placement, cells, kappa, below, above, packed, sides, strips, turned, facing,
    load_sem, edge_send, edge_recv, side_send, side_recv, strip_send, strip_recv,
    turn_send, turn_recv, ready,
):
    region = lax.axis_index("region")
    ax = lax.axis_index("ax")
    az = lax.axis_index("az")
    n_az = lax.axis_size("az")
    n_ax = lax.axis_size("ax")
    radial = state.shape[1]
    rows = radial // chunks
    is_vapor = region == 0
    nxt = lax.rem(az + 1, n_az)
    prv = lax.rem(az + n_az - 1, n_az)
    odd = lax.rem(ax, 2) == 1
    has_left = ax > 0
    has_right = ax < n_ax - 1
    is_worker = az < 4
    order = 2 * az + region
    iface = jnp.where(is_vapor, radial - 1, 0)
    next_later = jnp.logical_and(az != 11, az != 15)
    prev_later = jnp.logical_or(az == 0, az == 12)
    next_first = jnp.logical_not(next_later)
    prev_first = jnp.logical_not(prev_later)

    def signal(sem, **device):
        pl.semaphore_signal(sem, inc=1, device_id=device, device_id_type=MESH)

    def remote(src, dst, send, recv, **device):
        return pltpu.make_async_remote_copy(
            src_ref=src, dst_ref=dst, send_sem=send, recv_sem=recv,
            device_id=device, device_id_type=MESH,
        )

    barrier = pltpu.get_barrier_semaphore()
    pl.when(next_later)(lambda: signal(barrier, az=nxt))
    pl.when(prev_later)(lambda: signal(barrier, az=prv))
    pl.when(odd)(lambda: signal(barrier, ax=ax - 1))
    pl.when(jnp.logical_and(odd, has_right))(lambda: signal(barrier, ax=ax + 1))

    load_cells = pltpu.make_async_copy(state, cells, load_sem.at[0])
    load_kappa = pltpu.make_async_copy(conduct, kappa, load_sem.at[1])
    load_zones = pltpu.make_async_copy(zone_ref, zones, load_sem.at[2])
    load_place = pltpu.make_async_copy(place_ref, placement, load_sem.at[3])
    loads = [load_cells, load_kappa, load_zones, load_place]
    for c in loads:
        c.start()

    @pl.when(is_worker)
    def _():
        for other in range(8):
            pl.when(other > order)(
                functools.partial(signal, barrier, az=other // 2, region=other % 2)
            )

        @pl.loop(4, n_az)
        def _(j):
            signal(barrier, az=j, region=0)
            signal(barrier, az=j, region=1)

    count = (
        next_first.astype(jnp.int32)
        + prev_first.astype(jnp.int32)
        + jnp.where(odd, 0, 1 + has_left.astype(jnp.int32))
        + jnp.minimum(order, 8)
    )
    pl.when(count > 0)(lambda: pl.semaphore_wait(barrier, count))

    pl.when(next_first)(lambda: signal(ready.at[1], az=nxt))
    pl.when(prev_first)(lambda: signal(ready.at[0], az=prv))

    strip_copies = []
    for q in range(4):
        field = 1 - region if q < 2 else 2
        strip_copies.append(
            remote(
                state.at[field, iface, :, pl.ds(128 * (q % 2), 128)],
                strips.at[az],
                strip_send,
                strip_recv,
                az=q,
                region=1 - region,
            )
        )

    @pl.when(jnp.logical_not(is_worker))
    def _():
        for c in strip_copies:
            c.start()

    up, down = [], []
    for c in range(chunks):
        part = pl.ds(c * rows, rows)
        up.append(
            remote(
                state.at[:, part, pl.ds(7, 1), :], below.at[:, part],
                edge_send.at[0, c], edge_recv.at[0, c], az=nxt,
            )
        )
        down.append(
            remote(
                state.at[:, part, pl.ds(0, 1), :], above.at[:, part],
                edge_send.at[1, c], edge_recv.at[1, c], az=prv,
            )
        )

    def start_all(copies):
        for c in copies:
            c.start()

    @pl.when(next_first)
    def _():
        start_all(up)

    @pl.when(prev_first)
    def _():
        start_all(down)

    @pl.when(jnp.logical_not(odd))
    def _():
        signal(ready.at[2], ax=ax + 1)
        pl.when(has_left)(lambda: signal(ready.at[3], ax=ax - 1))

    @pl.when(jnp.logical_not(is_worker))
    def _():
        for q in range(4):
            signal(ready.at[4], az=q)

    @pl.when(is_worker)
    def _():
        for other in range(8):
            @pl.when(other < order)
            def _():
                same = region == other % 2
                pl.when(same)(functools.partial(signal, ready.at[4], az=other // 2))
                pl.when(jnp.logical_not(same))(
                    functools.partial(
                        signal, ready.at[5], az=other // 2, region=other % 2
                    )
                )

    @pl.when(next_later)
    def _():
        pl.semaphore_wait(ready.at[0], 1)
        start_all(up)

    @pl.when(is_worker)
    def _():
        later = jnp.where(is_vapor, 4 - az, 3 - az)
        pl.when(later > 0)(lambda: pl.semaphore_wait(ready.at[5], later))
        for c in strip_copies:
            c.start()

    for c in loads:
        c.wait()

    lane = lax.broadcasted_iota(jnp.int32, (8, 128), 1)
    first_lane = lane == 0
    last_lane = lane == 127
    sub = lax.broadcasted_iota(jnp.int32, (8, 128), 0)
    first_row = sub == 0
    last_row = sub == 7

    def pack(r, held):
        mine = lane == r
        got = []
        for f in range(3):
            left = pltpu.roll(cells[f, r, :, :128], r, 1)
            right = pltpu.roll(cells[f, r, :, 128:], lax.rem(r + 1, 128), 1)
            got.append(jnp.where(mine, left, held[2 * f]))
            got.append(jnp.where(mine, right, held[2 * f + 1]))
        return tuple(got)

    columns = lax.fori_loop(
        0, radial, pack, tuple(jnp.zeros((8, 128), jnp.float32) for _ in range(6)), unroll=4
    )
    for f in range(3):
        packed[0, f] = columns[2 * f]
        packed[1, f] = columns[2 * f + 1]

    to_left = remote(packed.at[0], sides.at[1], side_send.at[0], side_recv.at[1], ax=ax - 1)
    to_right = remote(packed.at[1], sides.at[0], side_send.at[1], side_recv.at[0], ax=ax + 1)

    @pl.when(has_left)
    def _():
        pl.when(odd)(lambda: pl.semaphore_wait(ready.at[2], 1))
        to_left.start()

    @pl.when(has_right)
    def _():
        pl.when(odd)(lambda: pl.semaphore_wait(ready.at[3], 1))
        to_right.start()

    @pl.when(prev_later)
    def _():
        pl.semaphore_wait(ready.at[1], 1)
        start_all(down)

    turn_copies = [
        remote(turned.at[j], facing.at[az], turn_send, turn_recv.at[az], az=j)
        for j in range(16)
    ]

    @pl.when(is_worker)
    def _():
        remote(strips, strips, strip_send, strip_recv, az=az).wait_recv()
        half = lax.rem(az, 2)
        shift = placement[pl.ds(half, 1), :]
        shift = jnp.where(is_vapor, shift, lax.rem(128 - shift, 128))
        circle = strips[...].reshape(128, 128)
        for bit in range(7):
            step = 1 << bit
            if step < 8:
                rolled = pltpu.roll(circle, 128 - step, 0)
            else:
                rolled = jnp.concatenate([circle[step:], circle[:step]], axis=0)
            circle = jnp.where(lax.rem(lax.div(shift, step), 2) == 1, rolled, circle)
        turned[...] = circle.reshape(16, 8, 128)
        facing[az] = turned[az]
        pl.semaphore_wait(ready.at[4], 15 - az)
        for j in range(16):
            pl.when(j != az)(turn_copies[j].start)

    @pl.when(has_left)
    def _():
        to_right.wait_recv()

    @pl.when(jnp.logical_not(has_left))
    def _():
        sides[0] = jnp.zeros((3, 8, 128), jnp.float32)

    @pl.when(has_right)
    def _():
        to_left.wait_recv()

    @pl.when(jnp.logical_not(has_right))
    def _():
        sides[1] = jnp.zeros((3, 8, 128), jnp.float32)

    def pick(vapor, wick):
        return jnp.where(is_vapor, jnp.float32(vapor), jnp.float32(wick))

    press = pick(1.0, 0.6)
    visc = pick(0.3, 0.05)
    fric = pick(0.1, 2.0)
    sound = pick(1.5, 0.8)
    pdiff = pick(0.2, 0.4)
    advect = pick(1.0, 0.5)

    def cell_row(r):
        inner = jnp.maximum(r - 1, 0)
        outer = jnp.minimum(r + 1, radial - 1)
        to_last = lax.rem(255 - r, 128)
        to_first = lax.rem(128 - r, 128)
        center, laplace, gradient = [], [], []
        for f in range(3):
            c = [cells[f, r, :, :128], cells[f, r, :, 128:]]
            plus = [pltpu.roll(c[0], 127, 1), pltpu.roll(c[1], 127, 1)]
            minus = [pltpu.roll(c[0], 1, 1), pltpu.roll(c[1], 1, 1)]
            from_right = pltpu.roll(sides[1, f], to_last, 1)
            from_left = pltpu.roll(sides[0, f], to_first, 1)
            ax_plus = [
                jnp.where(last_lane, plus[1], plus[0]),
                jnp.where(last_lane, from_right, plus[1]),
            ]
            ax_minus = [
                jnp.where(first_lane, from_left, minus[0]),
                jnp.where(first_lane, minus[0], minus[1]),
            ]
            laps, grads = [], []
            for h in range(2):
                lanes = pl.ds(128 * h, 128)
                az_plus = jnp.where(
                    last_row, above[f, r, :, lanes], pltpu.roll(c[h], 7, 0)
                )
                az_minus = jnp.where(
                    first_row, below[f, r, :, lanes], pltpu.roll(c[h], 1, 0)
                )
                laps.append(
                    cells[f, outer, :, lanes] + cells[f, inner, :, lanes]
                    + az_plus + az_minus + ax_plus[h] + ax_minus[h] - 6.0 * c[h]
                )
                grads.append(0.5 * (ax_plus[h] - ax_minus[h]))
            center.append(c)
            laplace.append(laps)
            gradient.append(grads)
        for h in range(2):
            lanes = pl.ds(128 * h, 128)
            t, p, u = center[0][h], center[1][h], center[2][h]
            out[0, r, :, lanes] = t + dt * (
                kappa[r, :, lanes] * laplace[0][h] - advect * u * gradient[0][h]
            )
            out[1, r, :, lanes] = p + dt * (
                -sound * gradient[2][h] + pdiff * laplace[1][h]
            )
            out[2, r, :, lanes] = u + dt * (
                -press * gradient[1][h] + visc * laplace[2][h] - fric * u
            )

    for c in range(chunks):
        up[c].wait_recv()
        down[c].wait_recv()

        @pl.loop(0, rows // unroll)
        def _(i):
            for k in range(unroll):
                cell_row(c * rows + i * unroll + k)

    for q in range(4):
        pl.when(az != q)(
            remote(facing.at[q], facing.at[q], turn_send, turn_recv.at[q], az=q).wait_recv
        )

    for h in range(2):
        lanes = pl.ds(128 * h, 128)
        own_t, own_p, own_u = [cells[f, iface, :, lanes] for f in range(3)]
        first, second = facing[h], facing[2 + h]
        t_wick = jnp.where(is_vapor, first, own_t)
        p_vapor = jnp.where(is_vapor, own_p, first)
        u_vapor = jnp.where(is_vapor, own_u, second)
        u_wick = jnp.where(is_vapor, second, own_u)
        evap = 2.0 * (t_wick - 0.5 * p_vapor)
        shear = 1.5 * (u_vapor - u_wick)
        out[0, iface, :, lanes] += dt * jnp.where(is_vapor, 0.5 * evap, -evap)
        out[1, iface, :, lanes] += dt * jnp.where(is_vapor, evap, -0.5 * evap)
        out[2, iface, :, lanes] += dt * jnp.where(is_vapor, -shear, 0.5 * shear)
        zone = jnp.broadcast_to(zones[pl.ds(h, 1), :], (8, 128))
        wall = cells[0, radial - 1, :, lanes]
        heat = jnp.where(
            zone == 0, jnp.float32(2.0), jnp.where(zone == 2, -1.5 * (wall + 1.0), 0.0)
        )
        out[0, radial - 1, :, lanes] += dt * jnp.where(is_vapor, 0.0, heat)

    for c in range(chunks):
        up[c].wait_send()
        down[c].wait_send()
    pl.when(has_left)(to_left.wait_send)
    pl.when(has_right)(to_right.wait_send)
    four = strips.at[pl.ds(0, 4)]
    remote(four, four, strip_send, strip_recv, az=az).wait_send()

    @pl.when(is_worker)
    def _():
        rest = turned.at[pl.ds(0, 15)]
        remote(rest, rest, turn_send, turn_recv.at[0], az=az).wait_send()


def store_kernel(new, out, sems):
    copies = [
        pltpu.make_async_copy(new.at[f], out.at[f], sems.at[f]) for f in range(3)
    ]
    for c in copies:
        c.start()
    for c in copies:
        c.wait()


def on_device(state, conduct, zones, placement):
    fields = state[0]
    f32 = jnp.float32
    shape = fields.shape
    radial, az_cells, ax_cells = shape[1:]
    hbm = pl.BlockSpec(memory_space=pltpu.HBM)
    vmem = pl.BlockSpec(memory_space=pltpu.VMEM)
    dma = pltpu.SemaphoreType.DMA
    new = pl.pallas_call(
        step_kernel,
        out_shape=jax.ShapeDtypeStruct(shape, f32),
        in_specs=[hbm] * 4,
        out_specs=vmem,
        scratch_shapes=[
            pltpu.VMEM((2, 128), jnp.int32),
            pltpu.VMEM((2, 128), jnp.int32),
            pltpu.VMEM(shape, f32),
            pltpu.VMEM(shape[1:], f32),
            pltpu.VMEM((3, radial, 1, ax_cells), f32),
            pltpu.VMEM((3, radial, 1, ax_cells), f32),
            pltpu.VMEM((2, 3, 8, 128), f32),
            pltpu.VMEM((2, 3, 8, 128), f32),
            pltpu.VMEM((16, 8, 128), f32),
            pltpu.VMEM((16, 8, 128), f32),
            pltpu.VMEM((4, 8, 128), f32),
            dma((4,)),
            dma((2, chunks)),
            dma((2, chunks)),
            dma((2,)),
            dma((2,)),
            dma,
            dma,
            dma,
            dma((4,)),
            pltpu.SemaphoreType.REGULAR((6,)),
        ],
        compiler_params=pltpu.CompilerParams(
            collective_id=0, has_side_effects=True, vmem_limit_bytes=60 << 20
        ),
        cost_estimate=pl.CostEstimate(
            flops=40 * fields.size, bytes_accessed=4 * 7 * conduct.size, transcendentals=0
        ),
    )(fields, conduct[0], zones.reshape(2, 128), placement.reshape(2, 128))
    result = pl.pallas_call(
        store_kernel,
        out_shape=jax.ShapeDtypeStruct(shape, f32),
        in_specs=[vmem],
        out_specs=hbm,
        scratch_shapes=[dma((3,))],
    )(new)
    return result[None]


def solution(mesh):
    return jax.shard_map(
        on_device,
        mesh=mesh,
        in_specs=(
            P("region", None, None, "az", "ax"),
            P("region", None, "az", "ax"),
            P("ax"),
            P("ax"),
        ),
        out_specs=P("region", None, None, "az", "ax"),
        check_vma=False,
    )
```

time: 83.6 us -> 33.8 us (0.40)
  the two profiles are of different devices: /device:TPU:1 before, /device:TPU:36 now
where the time goes in v1:
time: 33.8 us; the launch traced here: 33.7 us
  Pallas kernels  33.7 us (100%)
    pallas_call x1, Pallas kernels, on_device(): pl.pallas_call(step_kernel, out_shape=jax.ShapeDtypeStruct(shape, f32), i...  30.1 us
    pallas_call x1, Pallas kernels, on_device(): pl.pallas_call(store_kernel, out_shape=jax.ShapeDtypeStruct(shape, f32),...  3.57 us

profile of v1, /device:TPU:36, one launch (start us, length us, event | category | flops | bytes accessed | tf_op | source)
XLA Modules:
  0.0 33.7 jit_solution(7164223886134019171)
XLA Ops:
  0.0 30.1 %shard_map.46.new = f32[3,128,8,256]{3,2,1,0:T(8,128)} custom-call(f32[3,128,8,256]{3,2,1,0:T(8,128)} %bitcast.5, f32[128,8,256]{2,1,0:T(8,128)} %bitcast.6, s32[2,128]{1,0:T(2,128)} %bitcast.7, s32[2,128]{1,0:T(2,128)} %bitcast.8), custom_call_target="tpu_custom_call" | custom-call | flops 31457280 | bytes 7340032 | tf_op jit(solution)/shard_map/pallas_call | solution.py:382
  30.1 3.6 %shard_map.47 = f32[3,128,8,256]{3,2,1,0:T(8,128)} custom-call(f32[3,128,8,256]{3,2,1,0:T(8,128)} %shard_map.46.new), custom_call_target="tpu_custom_call" | custom-call | tf_op jit(solution)/shard_map/pallas_call | solution.py:417

commit v2 on v1

--- a/solution.py
+++ b/solution.py
@@ -381,7 +381,7 @@
     dma = pltpu.SemaphoreType.DMA
     new = pl.pallas_call(
         step_kernel,
-        out_shape=jax.ShapeDtypeStruct(shape, f32),
+        out_shape=pltpu.VMEM(shape, f32),
         in_specs=[hbm] * 4,
         out_specs=vmem,
         scratch_shapes=[
@@ -408,19 +408,23 @@
             pltpu.SemaphoreType.REGULAR((6,)),
         ],
         compiler_params=pltpu.CompilerParams(
-            collective_id=0, has_side_effects=True, vmem_limit_bytes=60 << 20
+            collective_id=0, has_side_effects=True, vmem_limit_bytes=24 << 20
         ),
         cost_estimate=pl.CostEstimate(
             flops=40 * fields.size, bytes_accessed=4 * 7 * conduct.size, transcendentals=0
         ),
-    )(fields, conduct[0], zones.reshape(2, 128), placement.reshape(2, 128))
+    )(*(
+        pltpu.with_memory_space_constraint(x, pltpu.HBM)
+        for x in (fields, conduct[0], zones.reshape(2, 128), placement.reshape(2, 128))
+    ))
     result = pl.pallas_call(
         store_kernel,
         out_shape=jax.ShapeDtypeStruct(shape, f32),
         in_specs=[vmem],
         out_specs=hbm,
         scratch_shapes=[dma((3,))],
-    )(new)
+        compiler_params=pltpu.CompilerParams(vmem_limit_bytes=1 << 20),
+    )(pltpu.with_memory_space_constraint(new, pltpu.VMEM))
     return result[None]
 
 

time: 33.8 us -> 30.2 us (0.89)
  Pallas kernels: 33.7 us -> 30.1 us
    pallas_call x1, Pallas kernels: 3.57 us -> 1.69 us  [on_device(): pl.pallas_call(store_kernel, out_shape=jax.ShapeDtypeStruct(shape, f32),...]
    pallas_call x1, Pallas kernels: 30.1 us -> 28.5 us  [on_device(): pl.pallas_call(step_kernel, out_shape=pltpu.VMEM(shape, f32), in_specs=[h...]
where the time goes in v2:
time: 30.2 us; the launch traced here: 30.1 us
  Pallas kernels  30.1 us (100%)
    pallas_call x1, Pallas kernels, on_device(): pl.pallas_call(step_kernel, out_shape=pltpu.VMEM(shape, f32), in_specs=[h...  28.5 us
    pallas_call x1, Pallas kernels, on_device(): pl.pallas_call(store_kernel, out_shape=jax.ShapeDtypeStruct(shape, f32),...  1.69 us

profile of v2, /device:TPU:36, one launch (start us, length us, event | category | flops | bytes accessed | tf_op | source)
XLA Modules:
  0.0 30.1 jit_solution(9018431050594674804)
XLA Ops:
  0.0 28.5 %shard_map.46.new = f32[3,128,8,256]{3,2,1,0:T(8,128)S(1)} custom-call(f32[3,128,8,256]{3,2,1,0:T(8,128)} %bitcast.5, f32[128,8,256]{2,1,0:T(8,128)} %bitcast.6, s32[2,128]{1,0:T(2,128)} %bitcast.7, s32[2,128]{1,0:T(2,128)} %bitcast.8), custom_call_target="tpu_custom_call" | custom-call | flops 31457280 | bytes 7340032 | tf_op jit(solution)/shard_map/pallas_call | solution.py:382
  28.5 1.7 %shard_map.47 = f32[3,128,8,256]{3,2,1,0:T(8,128)} custom-call(f32[3,128,8,256]{3,2,1,0:T(8,128)S(1)} %shard_map.46.new), custom_call_target="tpu_custom_call" | custom-call | tf_op jit(solution)/shard_map/pallas_call | solution.py:420

commit v3 on v2

--- a/solution.py
+++ b/solution.py
@@ -9,14 +9,14 @@
 MESH = pl.DeviceIdType.MESH
 dt = 0.05
 chunks = 8
-unroll = 4
+unroll = 8
 
 
 def step_kernel(
     state, conduct, zone_ref, place_ref, out,
-    zones, placement, cells, kappa, below, above, packed, sides, strips, turned, facing,
-    load_sem, edge_send, edge_recv, side_send, side_recv, strip_send, strip_recv,
-    turn_send, turn_recv, ready,
+    zones, placement, cells, kappa, edges, hop, packed, sides, strips, turned, facing,
+    load_sem, edge_send, edge_recv, hop_send, hop_recv, side_send, side_recv,
+    strip_send, strip_recv, turn_send, turn_recv, ready,
 ):
     region = lax.axis_index("region")
     ax = lax.axis_index("ax")
@@ -26,18 +26,21 @@
     radial = state.shape[1]
     rows = radial // chunks
     is_vapor = region == 0
+    y = lax.rem(az, 4)
     nxt = lax.rem(az + 1, n_az)
     prv = lax.rem(az + n_az - 1, n_az)
     odd = lax.rem(ax, 2) == 1
     has_left = ax > 0
     has_right = ax < n_ax - 1
-    is_worker = az < 4
+    is_worker = jnp.logical_or(az == 1, az == 2)
     order = 2 * az + region
     iface = jnp.where(is_vapor, radial - 1, 0)
     next_later = jnp.logical_and(az != 11, az != 15)
     prev_later = jnp.logical_or(az == 0, az == 12)
     next_first = jnp.logical_not(next_later)
     prev_first = jnp.logical_not(prev_later)
+    y_first = y == 0
+    y_last = y == 3
 
     def signal(sem, **device):
         pl.semaphore_signal(sem, inc=1, device_id=device, device_id_type=MESH)
@@ -51,25 +54,29 @@
     barrier = pltpu.get_barrier_semaphore()
     pl.when(next_later)(lambda: signal(barrier, az=nxt))
     pl.when(prev_later)(lambda: signal(barrier, az=prv))
+    pl.when(y_first)(lambda: signal(barrier, az=az + 3))
     pl.when(odd)(lambda: signal(barrier, ax=ax - 1))
     pl.when(jnp.logical_and(odd, has_right))(lambda: signal(barrier, ax=ax + 1))
 
-    load_cells = pltpu.make_async_copy(state, cells, load_sem.at[0])
-    load_kappa = pltpu.make_async_copy(conduct, kappa, load_sem.at[1])
-    load_zones = pltpu.make_async_copy(zone_ref, zones, load_sem.at[2])
-    load_place = pltpu.make_async_copy(place_ref, placement, load_sem.at[3])
-    loads = [load_cells, load_kappa, load_zones, load_place]
+    loads = [
+        pltpu.make_async_copy(src, dst, load_sem.at[i])
+        for i, (src, dst) in enumerate(
+            ((state, cells), (conduct, kappa), (zone_ref, zones), (place_ref, placement))
+        )
+    ]
     for c in loads:
         c.start()
 
-    @pl.when(is_worker)
-    def _():
-        for other in range(8):
+    @pl.when(az < 3)
+    def _():
+        for other in range(2, 6):
             pl.when(other > order)(
                 functools.partial(signal, barrier, az=other // 2, region=other % 2)
             )
 
-        @pl.loop(4, n_az)
+    @pl.when(is_worker)
+    def _():
+        @pl.loop(3, n_az)
         def _(j):
             signal(barrier, az=j, region=0)
             signal(barrier, az=j, region=1)
@@ -77,92 +84,123 @@
     count = (
         next_first.astype(jnp.int32)
         + prev_first.astype(jnp.int32)
+        + y_last.astype(jnp.int32)
         + jnp.where(odd, 0, 1 + has_left.astype(jnp.int32))
-        + jnp.minimum(order, 8)
+        + jnp.where(az == 0, 0, jnp.where(is_worker, order, 4))
     )
     pl.when(count > 0)(lambda: pl.semaphore_wait(barrier, count))
 
     pl.when(next_first)(lambda: signal(ready.at[1], az=nxt))
     pl.when(prev_first)(lambda: signal(ready.at[0], az=prv))
-
-    strip_copies = []
-    for q in range(4):
-        field = 1 - region if q < 2 else 2
-        strip_copies.append(
-            remote(
-                state.at[field, iface, :, pl.ds(128 * (q % 2), 128)],
-                strips.at[az],
-                strip_send,
-                strip_recv,
-                az=q,
-                region=1 - region,
-            )
-        )
-
-    @pl.when(jnp.logical_not(is_worker))
+    pl.when(y_last)(lambda: signal(ready.at[6], az=az - 3))
+
+    strip_copies = [
+        remote(
+            state.at[1 - region if q == 0 else 2, iface],
+            strips.at[az],
+            strip_send,
+            strip_recv,
+            az=1 + q,
+            region=1 - region,
+        )
+        for q in range(2)
+    ]
+
+    @pl.when(az > 2)
     def _():
         for c in strip_copies:
             c.start()
 
-    up, down = [], []
-    for c in range(chunks):
-        part = pl.ds(c * rows, rows)
-        up.append(
-            remote(
-                state.at[:, part, pl.ds(7, 1), :], below.at[:, part],
-                edge_send.at[0, c], edge_recv.at[0, c], az=nxt,
-            )
-        )
-        down.append(
-            remote(
-                state.at[:, part, pl.ds(0, 1), :], above.at[:, part],
-                edge_send.at[1, c], edge_recv.at[1, c], az=prv,
-            )
-        )
-
-    def start_all(copies):
-        for c in copies:
-            c.start()
+    far = (y_last, y_first)
+    neighbour = (nxt, prv)
+    other_end = (az - 3, az + 3)
+
+    def edge_source(d, c):
+        return state.at[:, pl.ds(c * rows, rows), pl.ds(7 - 7 * d, 1), :]
+
+    def edge_copy(d, c):
+        return remote(
+            edge_source(d, c), edges.at[d, :, pl.ds(c * rows, rows)],
+            edge_send.at[d, c], edge_recv.at[d, c], az=neighbour[d],
+        )
+
+    def detour_copy(d, i):
+        c = 2 * i + 1
+        return remote(
+            edge_source(d, c), hop.at[i], edge_send.at[d, c], hop_recv.at[i], az=other_end[d]
+        )
+
+    def onward_copy(d, i):
+        c = 2 * i + 1
+        return remote(
+            hop.at[i], edges.at[d, :, pl.ds(c * rows, rows)],
+            hop_send.at[i], edge_recv.at[d, c],
+            az=lax.rem(az + (4 if d == 0 else n_az - 4), n_az),
+        )
+
+    def start_even(d):
+        @pl.loop(0, chunks // 2)
+        def _(i):
+            edge_copy(d, 2 * i).start()
+
+    def start_odd(d):
+        @pl.loop(0, chunks // 2)
+        def _(i):
+            pl.when(far[d])(lambda: detour_copy(d, i).start())
+            pl.when(jnp.logical_not(far[d]))(lambda: edge_copy(d, 2 * i + 1).start())
+
+    def start_both(d):
+        @pl.loop(0, chunks // 2)
+        def _(i):
+            pl.when(far[d])(lambda: detour_copy(d, i).start())
+            edge_copy(d, 2 * i).start()
+            pl.when(jnp.logical_not(far[d]))(lambda: edge_copy(d, 2 * i + 1).start())
+
+    def pass_on(i):
+        @pl.when(jnp.logical_or(y_first, y_last))
+        def _():
+            remote(hop.at[i], hop.at[i], hop_send.at[i], hop_recv.at[i], az=nxt).wait_recv()
+            pl.when(y_first)(lambda: onward_copy(0, i).start())
+            pl.when(y_last)(lambda: onward_copy(1, i).start())
 
     @pl.when(next_first)
     def _():
-        start_all(up)
-
-    @pl.when(prev_first)
-    def _():
-        start_all(down)
+        start_both(0)
+
+    @pl.when(jnp.logical_and(prev_first, jnp.logical_not(y_first)))
+    def _():
+        start_both(1)
+
+    @pl.when(jnp.logical_and(prev_first, y_first))
+    def _():
+        start_even(1)
 
     @pl.when(jnp.logical_not(odd))
     def _():
         signal(ready.at[2], ax=ax + 1)
         pl.when(has_left)(lambda: signal(ready.at[3], ax=ax - 1))
 
-    @pl.when(jnp.logical_not(is_worker))
-    def _():
-        for q in range(4):
-            signal(ready.at[4], az=q)
+    @pl.when(az > 2)
+    def _():
+        signal(ready.at[4], az=1)
+        signal(ready.at[4], az=2)
 
     @pl.when(is_worker)
     def _():
-        for other in range(8):
-            @pl.when(other < order)
-            def _():
-                same = region == other % 2
-                pl.when(same)(functools.partial(signal, ready.at[4], az=other // 2))
-                pl.when(jnp.logical_not(same))(
-                    functools.partial(
-                        signal, ready.at[5], az=other // 2, region=other % 2
-                    )
-                )
+        pl.when(az == 2)(lambda: signal(ready.at[4], az=1))
+        for other in range(5):
+            pl.when(jnp.logical_and(other < order, region != other % 2))(
+                functools.partial(signal, ready.at[5], az=other // 2, region=other % 2)
+            )
 
     @pl.when(next_later)
     def _():
         pl.semaphore_wait(ready.at[0], 1)
-        start_all(up)
-
-    @pl.when(is_worker)
-    def _():
-        later = jnp.where(is_vapor, 4 - az, 3 - az)
+        start_both(0)
+
+    @pl.when(az < 3)
+    def _():
+        later = jnp.where(az == 0, 2, 3 - az - region)
         pl.when(later > 0)(lambda: pl.semaphore_wait(ready.at[5], later))
         for c in strip_copies:
             c.start()
@@ -188,7 +226,7 @@
         return tuple(got)
 
     columns = lax.fori_loop(
-        0, radial, pack, tuple(jnp.zeros((8, 128), jnp.float32) for _ in range(6)), unroll=4
+        0, radial, pack, tuple(jnp.zeros((8, 128), jnp.float32) for _ in range(6)), unroll=8
     )
     for f in range(3):
         packed[0, f] = columns[2 * f]
@@ -207,35 +245,15 @@
         pl.when(odd)(lambda: pl.semaphore_wait(ready.at[3], 1))
         to_right.start()
 
-    @pl.when(prev_later)
-    def _():
+    @pl.when(jnp.logical_and(prev_first, y_first))
+    def _():
+        pl.semaphore_wait(ready.at[6], 1)
+        start_odd(1)
+
+    def start_late():
+        pl.semaphore_wait(ready.at[6], 1)
         pl.semaphore_wait(ready.at[1], 1)
-        start_all(down)
-
-    turn_copies = [
-        remote(turned.at[j], facing.at[az], turn_send, turn_recv.at[az], az=j)
-        for j in range(16)
-    ]
-
-    @pl.when(is_worker)
-    def _():
-        remote(strips, strips, strip_send, strip_recv, az=az).wait_recv()
-        half = lax.rem(az, 2)
-        shift = placement[pl.ds(half, 1), :]
-        shift = jnp.where(is_vapor, shift, lax.rem(128 - shift, 128))
-        circle = strips[...].reshape(128, 128)
-        for bit in range(7):
-            step = 1 << bit
-            if step < 8:
-                rolled = pltpu.roll(circle, 128 - step, 0)
-            else:
-                rolled = jnp.concatenate([circle[step:], circle[:step]], axis=0)
-            circle = jnp.where(lax.rem(lax.div(shift, step), 2) == 1, rolled, circle)
-        turned[...] = circle.reshape(16, 8, 128)
-        facing[az] = turned[az]
-        pl.semaphore_wait(ready.at[4], 15 - az)
-        for j in range(16):
-            pl.when(j != az)(turn_copies[j].start)
+        start_both(1)
 
     @pl.when(has_left)
     def _():
@@ -262,6 +280,7 @@
     sound = pick(1.5, 0.8)
     pdiff = pick(0.2, 0.4)
     advect = pick(1.0, 0.5)
+    zero = jnp.float32(0.0)
 
     def cell_row(r):
         inner = jnp.maximum(r - 1, 0)
@@ -286,12 +305,8 @@
             laps, grads = [], []
             for h in range(2):
                 lanes = pl.ds(128 * h, 128)
-                az_plus = jnp.where(
-                    last_row, above[f, r, :, lanes], pltpu.roll(c[h], 7, 0)
-                )
-                az_minus = jnp.where(
-                    first_row, below[f, r, :, lanes], pltpu.roll(c[h], 1, 0)
-                )
+                az_plus = jnp.where(last_row, zero, pltpu.roll(c[h], 7, 0))
+                az_minus = jnp.where(first_row, zero, pltpu.roll(c[h], 1, 0))
                 laps.append(
                     cells[f, outer, :, lanes] + cells[f, inner, :, lanes]
                     + az_plus + az_minus + ax_plus[h] + ax_minus[h] - 6.0 * c[h]
@@ -313,24 +328,90 @@
                 -press * gradient[1][h] + visc * laplace[2][h] - fric * u
             )
 
-    for c in range(chunks):
-        up[c].wait_recv()
-        down[c].wait_recv()
+    first_pass = jnp.logical_or(az == 11, az == 12)
+    last_pass = az == 3
+    ahead = first_pass.astype(jnp.int32)
+    pl.when(first_pass)(lambda: pass_on(0))
+    turns = radial // unroll
+
+    @pl.loop(0, turns)
+    def _(i):
+        for k in range(unroll):
+            cell_row(i * unroll + k)
+        quarter = lax.div(i + 1, turns // 4)
+
+        @pl.when(lax.rem(i + 1, turns // 4) == 0)
+        def _():
+            pl.when(jnp.logical_and(quarter < 4, jnp.logical_not(last_pass)))(
+                lambda: pass_on(quarter - 1 + ahead)
+            )
+            pl.when(jnp.logical_and(az == 12, quarter == 1))(start_late)
+
+    pl.when(az == 0)(start_late)
+    pl.when(jnp.logical_not(jnp.logical_or(first_pass, last_pass)))(lambda: pass_on(3))
+
+    @pl.when(last_pass)
+    def _():
+        for i in range(chunks // 2):
+            pass_on(i)
+
+    @pl.when(is_worker)
+    def _():
+        remote(strips, strips, strip_send, strip_recv, az=az).wait_recv()
+        for h in range(2):
+            shift = placement[pl.ds(h, 1), :]
+            shift = jnp.where(is_vapor, shift, lax.rem(128 - shift, 128))
+            circle = strips[:, :, pl.ds(128 * h, 128)].reshape(128, 128)
+            for bit in range(7):
+                step = 1 << bit
+                if step < 8:
+                    rolled = pltpu.roll(circle, 128 - step, 0)
+                else:
+                    rolled = jnp.concatenate([circle[step:], circle[:step]], axis=0)
+                circle = jnp.where(lax.rem(lax.div(shift, step), 2) == 1, rolled, circle)
+            turned[:, :, pl.ds(128 * h, 128)] = circle.reshape(16, 8, 128)
+        facing[az - 1] = turned[az]
+        pl.semaphore_wait(ready.at[4], 15 - az)
+
+        @pl.loop(0, 16)
+        def _(j):
+            @pl.when(j != az)
+            def _():
+                remote(
+                    turned.at[j], facing.at[az - 1], turn_send, turn_recv.at[az - 1], az=j
+                ).start()
+
+    weights = (None, pdiff, visc)
+
+    @pl.loop(0, chunks)
+    def _(c):
+        edge_copy(0, c).wait_recv()
+        edge_copy(1, c).wait_recv()
 
         @pl.loop(0, rows // unroll)
         def _(i):
             for k in range(unroll):
-                cell_row(c * rows + i * unroll + k)
-
-    for q in range(4):
-        pl.when(az != q)(
+                r = c * rows + i * unroll + k
+                for h in range(2):
+                    lanes = pl.ds(128 * h, 128)
+                    for f in range(3):
+                        beyond = jnp.where(
+                            last_row,
+                            edges[1, f, r, :, lanes],
+                            jnp.where(first_row, edges[0, f, r, :, lanes], zero),
+                        )
+                        weight = kappa[r, :, lanes] if f == 0 else weights[f]
+                        out[f, r, :, lanes] += dt * (weight * beyond)
+
+    for q in range(2):
+        pl.when(az != q + 1)(
             remote(facing.at[q], facing.at[q], turn_send, turn_recv.at[q], az=q).wait_recv
         )
 
     for h in range(2):
         lanes = pl.ds(128 * h, 128)
         own_t, own_p, own_u = [cells[f, iface, :, lanes] for f in range(3)]
-        first, second = facing[h], facing[2 + h]
+        first, second = facing[0, :, lanes], facing[1, :, lanes]
         t_wick = jnp.where(is_vapor, first, own_t)
         p_vapor = jnp.where(is_vapor, own_p, first)
         u_vapor = jnp.where(is_vapor, own_u, second)
@@ -347,13 +428,20 @@
         )
         out[0, radial - 1, :, lanes] += dt * jnp.where(is_vapor, 0.0, heat)
 
-    for c in range(chunks):
-        up[c].wait_send()
-        down[c].wait_send()
+    @pl.loop(0, chunks)
+    def _(c):
+        edge_copy(0, c).wait_send()
+        edge_copy(1, c).wait_send()
+
+    @pl.when(jnp.logical_or(y_first, y_last))
+    def _():
+        for i in range(chunks // 2):
+            onward_copy(0, i).wait_send()
+
     pl.when(has_left)(to_left.wait_send)
     pl.when(has_right)(to_right.wait_send)
-    four = strips.at[pl.ds(0, 4)]
-    remote(four, four, strip_send, strip_recv, az=az).wait_send()
+    two = strips.at[pl.ds(0, 2)]
+    remote(two, two, strip_send, strip_recv, az=az).wait_send()
 
     @pl.when(is_worker)
     def _():
@@ -389,23 +477,25 @@
             pltpu.VMEM((2, 128), jnp.int32),
             pltpu.VMEM(shape, f32),
             pltpu.VMEM(shape[1:], f32),
-            pltpu.VMEM((3, radial, 1, ax_cells), f32),
-            pltpu.VMEM((3, radial, 1, ax_cells), f32),
+            pltpu.VMEM((2, 3, radial, 1, ax_cells), f32),
+            pltpu.VMEM((chunks // 2, 3, radial // chunks, 1, ax_cells), f32),
             pltpu.VMEM((2, 3, 8, 128), f32),
             pltpu.VMEM((2, 3, 8, 128), f32),
-            pltpu.VMEM((16, 8, 128), f32),
-            pltpu.VMEM((16, 8, 128), f32),
-            pltpu.VMEM((4, 8, 128), f32),
+            pltpu.VMEM((16, 8, 256), f32),
+            pltpu.VMEM((16, 8, 256), f32),
+            pltpu.VMEM((2, 8, 256), f32),
             dma((4,)),
             dma((2, chunks)),
             dma((2, chunks)),
+            dma((chunks // 2,)),
+            dma((chunks // 2,)),
             dma((2,)),
             dma((2,)),
             dma,
             dma,
             dma,
-            dma((4,)),
-            pltpu.SemaphoreType.REGULAR((6,)),
+            dma((2,)),
+            pltpu.SemaphoreType.REGULAR((7,)),
         ],
         compiler_params=pltpu.CompilerParams(
             collective_id=0, has_side_effects=True, vmem_limit_bytes=24 << 20

time: 30.2 us -> 28 us (0.927)
  the two profiles are of different devices: /device:TPU:36 before, /device:TPU:26 now
where the time goes in v3:
time: 28 us; the launch traced here: 27.9 us
  Pallas kernels  27.9 us (100%)
    pallas_call x1, Pallas kernels, on_device(): pl.pallas_call(step_kernel, out_shape=pltpu.VMEM(shape, f32), in_specs=[h...  26.2 us
    pallas_call x1, Pallas kernels, on_device(): pl.pallas_call(store_kernel, out_shape=jax.ShapeDtypeStruct(shape, f32),...  1.69 us

profile of v3, /device:TPU:26, one launch (start us, length us, event | category | flops | bytes accessed | tf_op | source)
XLA Modules:
  0.0 27.9 jit_solution(5005081607115224569)
XLA Ops:
  0.0 26.2 %shard_map.46.new = f32[3,128,8,256]{3,2,1,0:T(8,128)S(1)} custom-call(f32[3,128,8,256]{3,2,1,0:T(8,128)} %bitcast.5, f32[128,8,256]{2,1,0:T(8,128)} %bitcast.6, s32[2,128]{1,0:T(2,128)} %bitcast.7, s32[2,128]{1,0:T(2,128)} %bitcast.8), custom_call_target="tpu_custom_call" | custom-call | flops 31457280 | bytes 7340032 | tf_op jit(solution)/shard_map/pallas_call | solution.py:470
  26.2 1.7 %shard_map.47 = f32[3,128,8,256]{3,2,1,0:T(8,128)} custom-call(f32[3,128,8,256]{3,2,1,0:T(8,128)S(1)} %shard_map.46.new), custom_call_target="tpu_custom_call" | custom-call | tf_op jit(solution)/shard_map/pallas_call | solution.py:510

commit v4 on v3

--- a/solution.py
+++ b/solution.py
@@ -9,13 +9,14 @@
 MESH = pl.DeviceIdType.MESH
 dt = 0.05
 chunks = 8
+detours = 6
 unroll = 8
 
 
 def step_kernel(
     state, conduct, zone_ref, place_ref, out,
-    zones, placement, cells, kappa, edges, hop, packed, sides, strips, turned, facing,
-    load_sem, edge_send, edge_recv, hop_send, hop_recv, side_send, side_recv,
+    zones, placement, cells, kappa, edges, hop, lift, packed, sides, strips, turned, facing,
+    load_sem, lift_send, lift_recv, edge_send, edge_recv, hop_send, hop_recv, side_send, side_recv,
     strip_send, strip_recv, turn_send, turn_recv, ready,
 ):
     region = lax.axis_index("region")
@@ -33,14 +34,16 @@
     has_left = ax > 0
     has_right = ax < n_ax - 1
     is_worker = jnp.logical_or(az == 1, az == 2)
-    order = 2 * az + region
     iface = jnp.where(is_vapor, radial - 1, 0)
-    next_later = jnp.logical_and(az != 11, az != 15)
-    prev_later = jnp.logical_or(az == 0, az == 12)
+    swap_low = jnp.logical_and(is_vapor, jnp.logical_or(az == 10, az == 14))
+    swap_high = jnp.logical_and(is_vapor, jnp.logical_or(az == 11, az == 15))
+    next_later = jnp.logical_not(jnp.logical_or(jnp.logical_or(az == 11, az == 15), swap_low))
+    prev_later = jnp.logical_or(jnp.logical_or(az == 0, az == 12), swap_high)
     next_first = jnp.logical_not(next_later)
     prev_first = jnp.logical_not(prev_later)
-    y_first = y == 0
-    y_last = y == 3
+    even = lax.rem(ax, 2) == 0
+    low_end = jnp.logical_and(y == 0, region == 1)
+    high_end = jnp.logical_and(y == 3, region == 1)
 
     def signal(sem, **device):
         pl.semaphore_signal(sem, inc=1, device_id=device, device_id_type=MESH)
@@ -54,9 +57,9 @@
     barrier = pltpu.get_barrier_semaphore()
     pl.when(next_later)(lambda: signal(barrier, az=nxt))
     pl.when(prev_later)(lambda: signal(barrier, az=prv))
-    pl.when(y_first)(lambda: signal(barrier, az=az + 3))
-    pl.when(odd)(lambda: signal(barrier, ax=ax - 1))
-    pl.when(jnp.logical_and(odd, has_right))(lambda: signal(barrier, ax=ax + 1))
+    pl.when(low_end)(lambda: signal(barrier, az=az + 3))
+    pl.when(even)(lambda: signal(barrier, ax=ax + 1))
+    pl.when(jnp.logical_and(even, has_left))(lambda: signal(barrier, ax=ax - 1))
 
     loads = [
         pltpu.make_async_copy(src, dst, load_sem.at[i])
@@ -67,53 +70,74 @@
     for c in loads:
         c.start()
 
-    @pl.when(az < 3)
-    def _():
-        for other in range(2, 6):
-            pl.when(other > order)(
-                functools.partial(signal, barrier, az=other // 2, region=other % 2)
-            )
+    @pl.when(az < 2)
+    def _():
+        signal(barrier, az=2)
+        pl.when(az == 0)(lambda: signal(barrier, az=1))
 
     @pl.when(is_worker)
     def _():
+        pl.when(is_vapor)(lambda: signal(barrier, region=1))
+
         @pl.loop(3, n_az)
         def _(j):
-            signal(barrier, az=j, region=0)
-            signal(barrier, az=j, region=1)
+            signal(barrier, az=j)
 
     count = (
         next_first.astype(jnp.int32)
         + prev_first.astype(jnp.int32)
-        + y_last.astype(jnp.int32)
-        + jnp.where(odd, 0, 1 + has_left.astype(jnp.int32))
-        + jnp.where(az == 0, 0, jnp.where(is_worker, order, 4))
+        + high_end.astype(jnp.int32)
+        + jnp.where(odd, 1 + has_right.astype(jnp.int32), 0)
+        + jnp.minimum(az, 2)
+        + jnp.logical_and(is_worker, region == 1).astype(jnp.int32)
     )
     pl.when(count > 0)(lambda: pl.semaphore_wait(barrier, count))
 
     pl.when(next_first)(lambda: signal(ready.at[1], az=nxt))
     pl.when(prev_first)(lambda: signal(ready.at[0], az=prv))
-    pl.when(y_last)(lambda: signal(ready.at[6], az=az - 3))
+    pl.when(high_end)(lambda: signal(ready.at[6], az=az - 3))
+
+    def strip_source(q):
+        return state.at[1 - region if q == 0 else 2, iface]
 
     strip_copies = [
-        remote(
-            state.at[1 - region if q == 0 else 2, iface],
-            strips.at[az],
-            strip_send,
-            strip_recv,
-            az=1 + q,
-            region=1 - region,
-        )
+        remote(strip_source(q), strips.at[az], strip_send, strip_recv, az=1 + q)
         for q in range(2)
     ]
-
-    @pl.when(az > 2)
-    def _():
-        for c in strip_copies:
+    at_end = jnp.logical_and(region == 1, az > 3)
+    lifted_low = jnp.logical_and(at_end, y == 0)
+    lifted_high = jnp.logical_and(at_end, y == 3)
+    lifted = jnp.logical_or(lifted_low, lifted_high)
+    lifts = jnp.logical_and(at_end, jnp.logical_not(lifted))
+    lift_copies = [
+        remote(
+            strip_source(q), lift.at[q], lift_send.at[q], lift_recv.at[q],
+            az=jnp.where(lifted_low, az + 1, az - 1),
+        )
+        for q in range(2)
+    ]
+    lifted_copies = [
+        remote(
+            lift.at[q], strips.at[jnp.where(y == 1, az - 1, lax.rem(az + 1, n_az))],
+            lift_send.at[q], strip_recv, az=1 + q,
+        )
+        for q in range(2)
+    ]
+
+    def start_all(copies):
+        for c in copies:
             c.start()
 
-    far = (y_last, y_first)
+    def pass_strips():
+        for q in range(2):
+            lift_copies[q].wait_recv()
+            lifted_copies[q].start()
+
+    pl.when(jnp.logical_and(az > 2, jnp.logical_not(lifted)))(lambda: start_all(strip_copies))
+    pl.when(lifted_high)(lambda: start_all(lift_copies))
+
+    far = (high_end, low_end)
     neighbour = (nxt, prv)
-    other_end = (az - 3, az + 3)
 
     def edge_source(d, c):
         return state.at[:, pl.ds(c * rows, rows), pl.ds(7 - 7 * d, 1), :]
@@ -124,86 +148,59 @@
             edge_send.at[d, c], edge_recv.at[d, c], az=neighbour[d],
         )
 
-    def detour_copy(d, i):
-        c = 2 * i + 1
+    def detour_copy(d, c):
         return remote(
-            edge_source(d, c), hop.at[i], edge_send.at[d, c], hop_recv.at[i], az=other_end[d]
-        )
-
-    def onward_copy(d, i):
-        c = 2 * i + 1
+            edge_source(d, c), hop.at[c], edge_send.at[d, c], hop_recv.at[c], az=az + 6 * d - 3
+        )
+
+    def onward_copy(d, c):
         return remote(
-            hop.at[i], edges.at[d, :, pl.ds(c * rows, rows)],
-            hop_send.at[i], edge_recv.at[d, c],
+            hop.at[c], edges.at[d, :, pl.ds(c * rows, rows)], hop_send.at[c], edge_recv.at[d, c],
             az=lax.rem(az + (4 if d == 0 else n_az - 4), n_az),
         )
 
-    def start_even(d):
-        @pl.loop(0, chunks // 2)
-        def _(i):
-            edge_copy(d, 2 * i).start()
-
-    def start_odd(d):
-        @pl.loop(0, chunks // 2)
-        def _(i):
-            pl.when(far[d])(lambda: detour_copy(d, i).start())
-            pl.when(jnp.logical_not(far[d]))(lambda: edge_copy(d, 2 * i + 1).start())
-
-    def start_both(d):
-        @pl.loop(0, chunks // 2)
-        def _(i):
-            pl.when(far[d])(lambda: detour_copy(d, i).start())
-            edge_copy(d, 2 * i).start()
-            pl.when(jnp.logical_not(far[d]))(lambda: edge_copy(d, 2 * i + 1).start())
-
-    def pass_on(i):
-        @pl.when(jnp.logical_or(y_first, y_last))
+    def start(d):
+        @pl.loop(0, chunks)
+        def _(c):
+            round_about = jnp.logical_and(far[d], c < detours)
+            pl.when(round_about)(lambda: detour_copy(d, c).start())
+            pl.when(jnp.logical_not(round_about))(lambda: edge_copy(d, c).start())
+
+    def pass_on(first, last):
+        @pl.when(jnp.logical_or(low_end, high_end))
         def _():
-            remote(hop.at[i], hop.at[i], hop_send.at[i], hop_recv.at[i], az=nxt).wait_recv()
-            pl.when(y_first)(lambda: onward_copy(0, i).start())
-            pl.when(y_last)(lambda: onward_copy(1, i).start())
-
-    @pl.when(next_first)
-    def _():
-        start_both(0)
-
-    @pl.when(jnp.logical_and(prev_first, jnp.logical_not(y_first)))
-    def _():
-        start_both(1)
-
-    @pl.when(jnp.logical_and(prev_first, y_first))
-    def _():
-        start_even(1)
-
-    @pl.when(jnp.logical_not(odd))
-    def _():
-        signal(ready.at[2], ax=ax + 1)
-        pl.when(has_left)(lambda: signal(ready.at[3], ax=ax - 1))
-
-    @pl.when(az > 2)
-    def _():
-        signal(ready.at[4], az=1)
-        signal(ready.at[4], az=2)
+            @pl.loop(first, last)
+            def _(c):
+                remote(hop.at[c], hop.at[c], hop_send.at[c], hop_recv.at[c], az=nxt).wait_recv()
+                pl.when(low_end)(lambda: onward_copy(0, c).start())
+                pl.when(high_end)(lambda: onward_copy(1, c).start())
+
+    pl.when(next_first)(lambda: start(0))
+    pl.when(jnp.logical_and(prev_first, jnp.logical_not(low_end)))(lambda: start(1))
+
+    @pl.when(odd)
+    def _():
+        signal(ready.at[3], ax=ax - 1)
+        pl.when(has_right)(lambda: signal(ready.at[2], ax=ax + 1))
 
     @pl.when(is_worker)
     def _():
-        pl.when(az == 2)(lambda: signal(ready.at[4], az=1))
-        for other in range(5):
-            pl.when(jnp.logical_and(other < order, region != other % 2))(
-                functools.partial(signal, ready.at[5], az=other // 2, region=other % 2)
-            )
+        signal(ready.at[5], az=0)
+        pl.when(az == 2)(lambda: signal(ready.at[5], az=1))
+        pl.when(region == 1)(lambda: signal(ready.at[5], region=0))
 
     @pl.when(next_later)
     def _():
         pl.semaphore_wait(ready.at[0], 1)
-        start_both(0)
+        pl.when(lifted_low)(lambda: start_all(lift_copies))
+        start(0)
 
     @pl.when(az < 3)
     def _():
-        later = jnp.where(az == 0, 2, 3 - az - region)
+        later = jnp.where(az == 0, 2, 2 - az + jnp.where(is_vapor, 1, 0))
         pl.when(later > 0)(lambda: pl.semaphore_wait(ready.at[5], later))
-        for c in strip_copies:
-            c.start()
+        for q in range(2):
+            pl.when(az != 1 + q)(strip_copies[q].start)
 
     for c in loads:
         c.wait()
@@ -237,23 +234,24 @@
 
     @pl.when(has_left)
     def _():
-        pl.when(odd)(lambda: pl.semaphore_wait(ready.at[2], 1))
+        pl.when(even)(lambda: pl.semaphore_wait(ready.at[2], 1))
         to_left.start()
 
     @pl.when(has_right)
     def _():
-        pl.when(odd)(lambda: pl.semaphore_wait(ready.at[3], 1))
+        pl.when(even)(lambda: pl.semaphore_wait(ready.at[3], 1))
         to_right.start()
 
-    @pl.when(jnp.logical_and(prev_first, y_first))
+    @pl.when(low_end)
     def _():
         pl.semaphore_wait(ready.at[6], 1)
-        start_odd(1)
+        pl.when(prev_first)(lambda: start(1))
 
     def start_late():
-        pl.semaphore_wait(ready.at[6], 1)
         pl.semaphore_wait(ready.at[1], 1)
-        start_both(1)
+        start(1)
+
+    pl.when(swap_high)(start_late)
 
     @pl.when(has_left)
     def _():
@@ -328,39 +326,32 @@
                 -press * gradient[1][h] + visc * laplace[2][h] - fric * u
             )
 
-    first_pass = jnp.logical_or(az == 11, az == 12)
-    last_pass = az == 3
-    ahead = first_pass.astype(jnp.int32)
-    pl.when(first_pass)(lambda: pass_on(0))
     turns = radial // unroll
 
     @pl.loop(0, turns)
     def _(i):
         for k in range(unroll):
             cell_row(i * unroll + k)
-        quarter = lax.div(i + 1, turns // 4)
-
-        @pl.when(lax.rem(i + 1, turns // 4) == 0)
-        def _():
-            pl.when(jnp.logical_and(quarter < 4, jnp.logical_not(last_pass)))(
-                lambda: pass_on(quarter - 1 + ahead)
-            )
-            pl.when(jnp.logical_and(az == 12, quarter == 1))(start_late)
-
-    pl.when(az == 0)(start_late)
-    pl.when(jnp.logical_not(jnp.logical_or(first_pass, last_pass)))(lambda: pass_on(3))
-
-    @pl.when(last_pass)
-    def _():
-        for i in range(chunks // 2):
-            pass_on(i)
+
+        pl.when(jnp.logical_and(az == 12, i == turns // 4 - 1))(start_late)
+        pl.when(jnp.logical_and(az == 0, i == 3 * turns // 4 - 1))(start_late)
+        pl.when(jnp.logical_and(lifts, i == turns // 2 - 1))(pass_strips)
+        pl.when(jnp.logical_and(az >= 8, i == turns // 2 - 1))(lambda: pass_on(0, 1))
+        pl.when(jnp.logical_and(az >= 4, i == 3 * turns // 4 - 1))(
+            lambda: pass_on((az >= 8).astype(jnp.int32), 3 - (az < 8).astype(jnp.int32))
+        )
+
+    pass_on(jnp.where(az < 4, 0, jnp.where(az < 8, 2, 3)), detours)
 
     @pl.when(is_worker)
     def _():
-        remote(strips, strips, strip_send, strip_recv, az=az).wait_recv()
+        strips[az] = jnp.where(az == 1, cells[1 - region, iface], cells[2, iface])
+        others = strips.at[pl.ds(0, 15)]
+        remote(others, others, strip_send, strip_recv, az=az).wait_recv()
+        signal(ready.at[4], region=1 - region)
         for h in range(2):
             shift = placement[pl.ds(h, 1), :]
-            shift = jnp.where(is_vapor, shift, lax.rem(128 - shift, 128))
+            shift = jnp.where(is_vapor, lax.rem(128 - shift, 128), shift)
             circle = strips[:, :, pl.ds(128 * h, 128)].reshape(128, 128)
             for bit in range(7):
                 step = 1 << bit
@@ -370,16 +361,14 @@
                     rolled = jnp.concatenate([circle[step:], circle[:step]], axis=0)
                 circle = jnp.where(lax.rem(lax.div(shift, step), 2) == 1, rolled, circle)
             turned[:, :, pl.ds(128 * h, 128)] = circle.reshape(16, 8, 128)
-        facing[az - 1] = turned[az]
-        pl.semaphore_wait(ready.at[4], 15 - az)
-
-        @pl.loop(0, 16)
+        pl.semaphore_wait(ready.at[4], 1)
+
+        @pl.loop(0, n_az)
         def _(j):
-            @pl.when(j != az)
-            def _():
-                remote(
-                    turned.at[j], facing.at[az - 1], turn_send, turn_recv.at[az - 1], az=j
-                ).start()
+            remote(
+                turned.at[j], facing.at[az - 1], turn_send, turn_recv.at[az - 1],
+                az=j, region=1 - region,
+            ).start()
 
     weights = (None, pdiff, visc)
 
@@ -404,9 +393,7 @@
                         out[f, r, :, lanes] += dt * (weight * beyond)
 
     for q in range(2):
-        pl.when(az != q + 1)(
-            remote(facing.at[q], facing.at[q], turn_send, turn_recv.at[q], az=q).wait_recv
-        )
+        remote(facing.at[q], facing.at[q], turn_send, turn_recv.at[q], az=q).wait_recv()
 
     for h in range(2):
         lanes = pl.ds(128 * h, 128)
@@ -433,20 +420,28 @@
         edge_copy(0, c).wait_send()
         edge_copy(1, c).wait_send()
 
-    @pl.when(jnp.logical_or(y_first, y_last))
-    def _():
-        for i in range(chunks // 2):
-            onward_copy(0, i).wait_send()
+    @pl.when(jnp.logical_or(low_end, high_end))
+    def _():
+        @pl.loop(0, detours)
+        def _(c):
+            onward_copy(0, c).wait_send()
 
     pl.when(has_left)(to_left.wait_send)
     pl.when(has_right)(to_right.wait_send)
-    two = strips.at[pl.ds(0, 2)]
-    remote(two, two, strip_send, strip_recv, az=az).wait_send()
-
     @pl.when(is_worker)
     def _():
-        rest = turned.at[pl.ds(0, 15)]
-        remote(rest, rest, turn_send, turn_recv.at[0], az=az).wait_send()
+        strip_copies[0].wait_send()
+        remote(turned, turned, turn_send, turn_recv.at[0], az=az).wait_send()
+
+    @pl.when(jnp.logical_not(jnp.logical_or(is_worker, lifted)))
+    def _():
+        two = facing
+        remote(two, two, strip_send, strip_recv, az=az).wait_send()
+
+    @pl.when(jnp.logical_or(lifted, lifts))
+    def _():
+        for c in lift_copies:
+            c.wait_send()
 
 
 def store_kernel(new, out, sems):
@@ -478,17 +473,20 @@
             pltpu.VMEM(shape, f32),
             pltpu.VMEM(shape[1:], f32),
             pltpu.VMEM((2, 3, radial, 1, ax_cells), f32),
-            pltpu.VMEM((chunks // 2, 3, radial // chunks, 1, ax_cells), f32),
+            pltpu.VMEM((detours, 3, radial // chunks, 1, ax_cells), f32),
+            pltpu.VMEM((2, 8, ax_cells), f32),
             pltpu.VMEM((2, 3, 8, 128), f32),
             pltpu.VMEM((2, 3, 8, 128), f32),
             pltpu.VMEM((16, 8, 256), f32),
             pltpu.VMEM((16, 8, 256), f32),
             pltpu.VMEM((2, 8, 256), f32),
             dma((4,)),
+            dma((2,)),
+            dma((2,)),
             dma((2, chunks)),
             dma((2, chunks)),
-            dma((chunks // 2,)),
-            dma((chunks // 2,)),
+            dma((detours,)),
+            dma((detours,)),
             dma((2,)),
             dma((2,)),
             dma,

time: 28 us -> 26.2 us (0.936)
  the two profiles are of different devices: /device:TPU:26 before, /device:TPU:1 now
where the time goes in v4:
time: 26.2 us; the launch traced here: 25.8 us
  Pallas kernels  25.8 us (98%)
    pallas_call x1, Pallas kernels, on_device(): pl.pallas_call(step_kernel, out_shape=pltpu.VMEM(shape, f32), in_specs=[h...  24.1 us
    pallas_call x1, Pallas kernels, on_device(): pl.pallas_call(store_kernel, out_shape=jax.ShapeDtypeStruct(shape, f32),...  1.69 us

profile of v4, /device:TPU:1, one launch (start us, length us, event | category | flops | bytes accessed | tf_op | source)
XLA Modules:
  0.0 25.8 jit_solution(9214140341732482870)
XLA Ops:
  0.0 24.1 %shard_map.46.new = f32[3,128,8,256]{3,2,1,0:T(8,128)S(1)} custom-call(f32[3,128,8,256]{3,2,1,0:T(8,128)} %bitcast.5, f32[128,8,256]{2,1,0:T(8,128)} %bitcast.6, s32[2,128]{1,0:T(2,128)} %bitcast.7, s32[2,128]{1,0:T(2,128)} %bitcast.8), custom_call_target="tpu_custom_call" | custom-call | flops 31457280 | bytes 7340032 | tf_op jit(solution)/shard_map/pallas_call | solution.py:465
  24.1 1.7 %shard_map.47 = f32[3,128,8,256]{3,2,1,0:T(8,128)} custom-call(f32[3,128,8,256]{3,2,1,0:T(8,128)S(1)} %shard_map.46.new), custom_call_target="tpu_custom_call" | custom-call | tf_op jit(solution)/shard_map/pallas_call | solution.py:508

commit v5 on v4

--- a/solution.py
+++ b/solution.py
@@ -35,9 +35,10 @@
     has_right = ax < n_ax - 1
     is_worker = jnp.logical_or(az == 1, az == 2)
     iface = jnp.where(is_vapor, radial - 1, 0)
-    swap_low = jnp.logical_and(is_vapor, jnp.logical_or(az == 10, az == 14))
-    swap_high = jnp.logical_and(is_vapor, jnp.logical_or(az == 11, az == 15))
-    next_later = jnp.logical_not(jnp.logical_or(jnp.logical_or(az == 11, az == 15), swap_low))
+    swap_high = jnp.logical_or(az == 11, az == 15)
+    next_later = jnp.logical_not(
+        jnp.logical_or(swap_high, jnp.logical_or(az == 10, az == 14))
+    )
     prev_later = jnp.logical_or(jnp.logical_or(az == 0, az == 12), swap_high)
     next_first = jnp.logical_not(next_later)
     prev_first = jnp.logical_not(prev_later)
@@ -97,6 +98,12 @@
     pl.when(prev_first)(lambda: signal(ready.at[0], az=prv))
     pl.when(high_end)(lambda: signal(ready.at[6], az=az - 3))
 
+    @pl.when(is_worker)
+    def _():
+        signal(ready.at[5], az=0)
+        pl.when(az == 2)(lambda: signal(ready.at[5], az=1))
+        pl.when(region == 1)(lambda: signal(ready.at[5], region=0))
+
     def strip_source(q):
         return state.at[1 - region if q == 0 else 2, iface]
 
@@ -104,23 +111,14 @@
         remote(strip_source(q), strips.at[az], strip_send, strip_recv, az=1 + q)
         for q in range(2)
     ]
-    at_end = jnp.logical_and(region == 1, az > 3)
-    lifted_low = jnp.logical_and(at_end, y == 0)
-    lifted_high = jnp.logical_and(at_end, y == 3)
-    lifted = jnp.logical_or(lifted_low, lifted_high)
-    lifts = jnp.logical_and(at_end, jnp.logical_not(lifted))
+    lifted = jnp.logical_and(region == 1, az == 15)
+    lifts = jnp.logical_and(region == 1, az == 12)
     lift_copies = [
-        remote(
-            strip_source(q), lift.at[q], lift_send.at[q], lift_recv.at[q],
-            az=jnp.where(lifted_low, az + 1, az - 1),
-        )
+        remote(strip_source(q), lift.at[q], lift_send.at[q], lift_recv.at[q], az=12)
         for q in range(2)
     ]
     lifted_copies = [
-        remote(
-            lift.at[q], strips.at[jnp.where(y == 1, az - 1, lax.rem(az + 1, n_az))],
-            lift_send.at[q], strip_recv, az=1 + q,
-        )
+        remote(lift.at[q], strips.at[15], lift_send.at[q], strip_recv, az=1 + q)
         for q in range(2)
     ]
 
@@ -134,7 +132,7 @@
             lifted_copies[q].start()
 
     pl.when(jnp.logical_and(az > 2, jnp.logical_not(lifted)))(lambda: start_all(strip_copies))
-    pl.when(lifted_high)(lambda: start_all(lift_copies))
+    pl.when(lifted)(lambda: start_all(lift_copies))
 
     far = (high_end, low_end)
     neighbour = (nxt, prv)
@@ -182,25 +180,6 @@
     def _():
         signal(ready.at[3], ax=ax - 1)
         pl.when(has_right)(lambda: signal(ready.at[2], ax=ax + 1))
-
-    @pl.when(is_worker)
-    def _():
-        signal(ready.at[5], az=0)
-        pl.when(az == 2)(lambda: signal(ready.at[5], az=1))
-        pl.when(region == 1)(lambda: signal(ready.at[5], region=0))
-
-    @pl.when(next_later)
-    def _():
-        pl.semaphore_wait(ready.at[0], 1)
-        pl.when(lifted_low)(lambda: start_all(lift_copies))
-        start(0)
-
-    @pl.when(az < 3)
-    def _():
-        later = jnp.where(az == 0, 2, 2 - az + jnp.where(is_vapor, 1, 0))
-        pl.when(later > 0)(lambda: pl.semaphore_wait(ready.at[5], later))
-        for q in range(2):
-            pl.when(az != 1 + q)(strip_copies[q].start)
 
     for c in loads:
         c.wait()
@@ -228,6 +207,18 @@
     for f in range(3):
         packed[0, f] = columns[2 * f]
         packed[1, f] = columns[2 * f + 1]
+
+    @pl.when(az < 3)
+    def _():
+        later = jnp.where(az == 0, 2, 2 - az + jnp.where(is_vapor, 1, 0))
+        pl.when(later > 0)(lambda: pl.semaphore_wait(ready.at[5], later))
+        for q in range(2):
+            pl.when(az != 1 + q)(strip_copies[q].start)
+
+    @pl.when(next_later)
+    def _():
+        pl.semaphore_wait(ready.at[0], 1)
+        start(0)
 
     to_left = remote(packed.at[0], sides.at[1], side_send.at[0], side_recv.at[1], ax=ax - 1)
     to_right = remote(packed.at[1], sides.at[0], side_send.at[1], side_recv.at[0], ax=ax + 1)
@@ -333,9 +324,9 @@
         for k in range(unroll):
             cell_row(i * unroll + k)
 
+        pl.when(jnp.logical_and(lifts, i == turns // 4 - 1))(pass_strips)
         pl.when(jnp.logical_and(az == 12, i == turns // 4 - 1))(start_late)
         pl.when(jnp.logical_and(az == 0, i == 3 * turns // 4 - 1))(start_late)
-        pl.when(jnp.logical_and(lifts, i == turns // 2 - 1))(pass_strips)
         pl.when(jnp.logical_and(az >= 8, i == turns // 2 - 1))(lambda: pass_on(0, 1))
         pl.when(jnp.logical_and(az >= 4, i == 3 * turns // 4 - 1))(
             lambda: pass_on((az >= 8).astype(jnp.int32), 3 - (az < 8).astype(jnp.int32))

time: 26.2 us -> 24.8 us (0.947); the launches traced: 25.8 us -> 24.7 us
  Pallas kernels: 25.8 us -> 24.7 us
    pallas_call x1, Pallas kernels: 24.1 us -> 23 us  [on_device(): pl.pallas_call(step_kernel, out_shape=pltpu.VMEM(shape, f32), in_specs=[h...]
where the time goes in v5:
time: 24.8 us; the launch traced here: 24.7 us
  Pallas kernels  24.7 us (100%)
    pallas_call x1, Pallas kernels, on_device(): pl.pallas_call(step_kernel, out_shape=pltpu.VMEM(shape, f32), in_specs=[h...  23 us
    pallas_call x1, Pallas kernels, on_device(): pl.pallas_call(store_kernel, out_shape=jax.ShapeDtypeStruct(shape, f32),...  1.69 us

profile of v5, /device:TPU:1, one launch (start us, length us, event | category | flops | bytes accessed | tf_op | source)
XLA Modules:
  0.0 24.7 jit_solution(1751109474554262880)
XLA Ops:
  0.0 23.0 %shard_map.46.new = f32[3,128,8,256]{3,2,1,0:T(8,128)S(1)} custom-call(f32[3,128,8,256]{3,2,1,0:T(8,128)} %bitcast.5, f32[128,8,256]{2,1,0:T(8,128)} %bitcast.6, s32[2,128]{1,0:T(2,128)} %bitcast.7, s32[2,128]{1,0:T(2,128)} %bitcast.8), custom_call_target="tpu_custom_call" | custom-call | flops 31457280 | bytes 7340032 | tf_op jit(solution)/shard_map/pallas_call | solution.py:456
  23.0 1.7 %shard_map.47 = f32[3,128,8,256]{3,2,1,0:T(8,128)} custom-call(f32[3,128,8,256]{3,2,1,0:T(8,128)S(1)} %shard_map.46.new), custom_call_target="tpu_custom_call" | custom-call | tf_op jit(solution)/shard_map/pallas_call | solution.py:499

commit v6 on v5

--- a/solution.py
+++ b/solution.py
@@ -9,7 +9,6 @@
 MESH = pl.DeviceIdType.MESH
 dt = 0.05
 chunks = 8
-detours = 6
 unroll = 8
 
 
@@ -45,6 +44,9 @@
     even = lax.rem(ax, 2) == 0
     low_end = jnp.logical_and(y == 0, region == 1)
     high_end = jnp.logical_and(y == 3, region == 1)
+    inner = jnp.logical_and(
+        region == 1, jnp.logical_or(az == 1, jnp.logical_or(az == 9, az == 13))
+    )
 
     def signal(sem, **device):
         pl.semaphore_signal(sem, inc=1, device_id=device, device_id_type=MESH)
@@ -59,6 +61,7 @@
     pl.when(next_later)(lambda: signal(barrier, az=nxt))
     pl.when(prev_later)(lambda: signal(barrier, az=prv))
     pl.when(low_end)(lambda: signal(barrier, az=az + 3))
+    pl.when(jnp.logical_and(inner, az > 8))(lambda: signal(barrier, az=az + 2))
     pl.when(even)(lambda: signal(barrier, ax=ax + 1))
     pl.when(jnp.logical_and(even, has_left))(lambda: signal(barrier, ax=ax - 1))
 
@@ -88,6 +91,7 @@
         next_first.astype(jnp.int32)
         + prev_first.astype(jnp.int32)
         + high_end.astype(jnp.int32)
+        + jnp.logical_and(high_end, az > 8).astype(jnp.int32)
         + jnp.where(odd, 1 + has_right.astype(jnp.int32), 0)
         + jnp.minimum(az, 2)
         + jnp.logical_and(is_worker, region == 1).astype(jnp.int32)
@@ -111,8 +115,8 @@
         remote(strip_source(q), strips.at[az], strip_send, strip_recv, az=1 + q)
         for q in range(2)
     ]
-    lifted = jnp.logical_and(region == 1, az == 15)
-    lifts = jnp.logical_and(region == 1, az == 12)
+    lifted = az < 0
+    lifts = az < 0
     lift_copies = [
         remote(strip_source(q), lift.at[q], lift_send.at[q], lift_recv.at[q], az=12)
         for q in range(2)
@@ -146,35 +150,53 @@
             edge_send.at[d, c], edge_recv.at[d, c], az=neighbour[d],
         )
 
+    round_about = (
+        jnp.where(az < 8, 6, 5),
+        jnp.where(az < 12, 5, 6),
+    )
+    rest_inner = (jnp.logical_and(high_end, az > 8), jnp.logical_and(low_end, az == 0))
+
     def detour_copy(d, c):
+        way = jnp.where(c < round_about[d], 3, 2 - d)
         return remote(
-            edge_source(d, c), hop.at[c], edge_send.at[d, c], hop_recv.at[c], az=az + 6 * d - 3
+            edge_source(d, c), hop.at[c], edge_send.at[d, c], hop_recv.at[c],
+            az=az - way if d == 0 else az + way,
         )
+
+    upward = jnp.logical_or(lax.rem(y, 2) == 0, jnp.logical_or(az == 9, az == 13))
+    onward_even = lax.rem(az + 4 - y, n_az)
+    onward_odd = lax.rem(az + n_az - 1 - y, n_az)
 
     def onward_copy(d, c):
         return remote(
             hop.at[c], edges.at[d, :, pl.ds(c * rows, rows)], hop_send.at[c], edge_recv.at[d, c],
-            az=lax.rem(az + (4 if d == 0 else n_az - 4), n_az),
+            az=onward_even if d == 0 else onward_odd,
         )
 
+    def start_part(d, first, last):
+        @pl.loop(first, last)
+        def _(c):
+            detour = jnp.logical_and(far[d], jnp.logical_or(c < round_about[d], rest_inner[d]))
+            pl.when(detour)(lambda: detour_copy(d, c).start())
+            pl.when(jnp.logical_not(detour))(lambda: edge_copy(d, c).start())
+
     def start(d):
-        @pl.loop(0, chunks)
-        def _(c):
-            round_about = jnp.logical_and(far[d], c < detours)
-            pl.when(round_about)(lambda: detour_copy(d, c).start())
-            pl.when(jnp.logical_not(round_about))(lambda: edge_copy(d, c).start())
+        start_part(d, 0, chunks)
 
     def pass_on(first, last):
-        @pl.when(jnp.logical_or(low_end, high_end))
+        @pl.when(region == 1)
         def _():
             @pl.loop(first, last)
             def _(c):
                 remote(hop.at[c], hop.at[c], hop_send.at[c], hop_recv.at[c], az=nxt).wait_recv()
-                pl.when(low_end)(lambda: onward_copy(0, c).start())
-                pl.when(high_end)(lambda: onward_copy(1, c).start())
-
-    pl.when(next_first)(lambda: start(0))
-    pl.when(jnp.logical_and(prev_first, jnp.logical_not(low_end)))(lambda: start(1))
+                pl.when(upward)(lambda: onward_copy(0, c).start())
+                pl.when(jnp.logical_not(upward))(lambda: onward_copy(1, c).start())
+
+    last_straight = jnp.logical_and(az == 15, is_vapor)
+    pl.when(jnp.logical_and(next_first, jnp.logical_not(last_straight)))(lambda: start(0))
+    pl.when(prev_first)(
+        lambda: start_part(1, jnp.where(low_end, round_about[1], 0), chunks)
+    )
 
     @pl.when(odd)
     def _():
@@ -183,6 +205,8 @@
 
     for c in loads:
         c.wait()
+
+    pl.when(last_straight)(lambda: start(0))
 
     lane = lax.broadcasted_iota(jnp.int32, (8, 128), 1)
     first_lane = lane == 0
@@ -236,7 +260,7 @@
     @pl.when(low_end)
     def _():
         pl.semaphore_wait(ready.at[6], 1)
-        pl.when(prev_first)(lambda: start(1))
+        pl.when(prev_first)(lambda: start_part(1, 0, round_about[1]))
 
     def start_late():
         pl.semaphore_wait(ready.at[1], 1)
@@ -318,6 +342,10 @@
             )
 
     turns = radial // unroll
+    at_end = jnp.logical_or(y == 0, y == 3)
+    busy = jnp.logical_and(
+        jnp.logical_and(at_end, az > 4), az < 15
+    )
 
     @pl.loop(0, turns)
     def _(i):
@@ -327,12 +355,20 @@
         pl.when(jnp.logical_and(lifts, i == turns // 4 - 1))(pass_strips)
         pl.when(jnp.logical_and(az == 12, i == turns // 4 - 1))(start_late)
         pl.when(jnp.logical_and(az == 0, i == 3 * turns // 4 - 1))(start_late)
-        pl.when(jnp.logical_and(az >= 8, i == turns // 2 - 1))(lambda: pass_on(0, 1))
-        pl.when(jnp.logical_and(az >= 4, i == 3 * turns // 4 - 1))(
-            lambda: pass_on((az >= 8).astype(jnp.int32), 3 - (az < 8).astype(jnp.int32))
-        )
-
-    pass_on(jnp.where(az < 4, 0, jnp.where(az < 8, 2, 3)), detours)
+        quarter = lax.div(i + 1, turns // 4)
+
+        @pl.when(lax.rem(i + 1, turns // 4) == 0)
+        def _():
+            pl.when(jnp.logical_and(busy, quarter < 4))(
+                lambda: pass_on(quarter - 1, jnp.where(quarter < 3, quarter, quarter + 1))
+            )
+            pl.when(jnp.logical_and(az == 15, quarter == 3))(lambda: pass_on(0, 1))
+            pl.when(jnp.logical_and(jnp.logical_and(inner, az > 8), quarter < 4))(
+                lambda: pass_on(round_about[0] + quarter - 1, round_about[0] + quarter)
+            )
+
+    mine = jnp.where(y == 0, round_about[0], round_about[1])
+    pl.when(at_end)(lambda: pass_on(jnp.where(busy, 4, (az == 15).astype(jnp.int32)), mine))
 
     @pl.when(is_worker)
     def _():
@@ -360,6 +396,8 @@
                 turned.at[j], facing.at[az - 1], turn_send, turn_recv.at[az - 1],
                 az=j, region=1 - region,
             ).start()
+
+    pl.when(jnp.logical_and(inner, az == 1))(lambda: pass_on(round_about[1], chunks))
 
     weights = (None, pdiff, visc)
 
@@ -411,9 +449,9 @@
         edge_copy(0, c).wait_send()
         edge_copy(1, c).wait_send()
 
-    @pl.when(jnp.logical_or(low_end, high_end))
-    def _():
-        @pl.loop(0, detours)
+    @pl.when(jnp.logical_or(inner, jnp.logical_and(region == 1, at_end)))
+    def _():
+        @pl.loop(jnp.where(at_end, 0, 5), jnp.where(at_end, mine, chunks))
         def _(c):
             onward_copy(0, c).wait_send()
 
@@ -464,7 +502,7 @@
             pltpu.VMEM(shape, f32),
             pltpu.VMEM(shape[1:], f32),
             pltpu.VMEM((2, 3, radial, 1, ax_cells), f32),
-            pltpu.VMEM((detours, 3, radial // chunks, 1, ax_cells), f32),
+            pltpu.VMEM((chunks, 3, radial // chunks, 1, ax_cells), f32),
             pltpu.VMEM((2, 8, ax_cells), f32),
             pltpu.VMEM((2, 3, 8, 128), f32),
             pltpu.VMEM((2, 3, 8, 128), f32),
@@ -476,8 +514,8 @@
             dma((2,)),
             dma((2, chunks)),
             dma((2, chunks)),
-            dma((detours,)),
-            dma((detours,)),
+            dma((chunks,)),
+            dma((chunks,)),
             dma((2,)),
             dma((2,)),
             dma,

time: 24.8 us -> 23.7 us (0.956)
  Pallas kernels: 24.7 us -> 23.7 us
    pallas_call x1, Pallas kernels: 23 us -> 22 us  [on_device(): pl.pallas_call(step_kernel, out_shape=pltpu.VMEM(shape, f32), in_specs=[h...]
where the time goes in v6:
time: 23.7 us
  Pallas kernels  23.7 us (100%)
    pallas_call x1, Pallas kernels, on_device(): pl.pallas_call(step_kernel, out_shape=pltpu.VMEM(shape, f32), in_specs=[h...  22 us
    pallas_call x1, Pallas kernels, on_device(): pl.pallas_call(store_kernel, out_shape=jax.ShapeDtypeStruct(shape, f32),...  1.69 us

profile of v6, /device:TPU:1, one launch (start us, length us, event | category | flops | bytes accessed | tf_op | source)
XLA Modules:
  0.0 23.7 jit_solution(8947689506739929083)
XLA Ops:
  0.0 22.0 %shard_map.46.new = f32[3,128,8,256]{3,2,1,0:T(8,128)S(1)} custom-call(f32[3,128,8,256]{3,2,1,0:T(8,128)} %bitcast.5, f32[128,8,256]{2,1,0:T(8,128)} %bitcast.6, s32[2,128]{1,0:T(2,128)} %bitcast.7, s32[2,128]{1,0:T(2,128)} %bitcast.8), custom_call_target="tpu_custom_call" | custom-call | flops 31457280 | bytes 7340032 | tf_op jit(solution)/shard_map/pallas_call | solution.py:494
  22.0 1.7 %shard_map.47 = f32[3,128,8,256]{3,2,1,0:T(8,128)} custom-call(f32[3,128,8,256]{3,2,1,0:T(8,128)S(1)} %shard_map.46.new), custom_call_target="tpu_custom_call" | custom-call | tf_op jit(solution)/shard_map/pallas_call | solution.py:537

commit v7 on v6

--- a/solution.py
+++ b/solution.py
@@ -14,7 +14,7 @@
 
 def step_kernel(
     state, conduct, zone_ref, place_ref, out,
-    zones, placement, cells, kappa, edges, hop, lift, packed, sides, strips, turned, facing,
+    zones, placement, cells, kappa, edges, hop, lift, packed, packed_in, sides, strips, turned, facing,
     load_sem, lift_send, lift_recv, edge_send, edge_recv, hop_send, hop_recv, side_send, side_recv,
     strip_send, strip_recv, turn_send, turn_recv, ready,
 ):
@@ -147,19 +147,19 @@
     def edge_copy(d, c):
         return remote(
             edge_source(d, c), edges.at[d, :, pl.ds(c * rows, rows)],
-            edge_send.at[d, c], edge_recv.at[d, c], az=neighbour[d],
+            edge_send.at[d], edge_recv.at[d, c], az=neighbour[d],
         )
 
     round_about = (
-        jnp.where(az < 8, 6, 5),
-        jnp.where(az < 12, 5, 6),
+        jnp.where(az < 8, 7, 5),
+        jnp.where(az < 4, 7, jnp.where(az < 12, 5, 6)),
     )
     rest_inner = (jnp.logical_and(high_end, az > 8), jnp.logical_and(low_end, az == 0))
 
     def detour_copy(d, c):
         way = jnp.where(c < round_about[d], 3, 2 - d)
         return remote(
-            edge_source(d, c), hop.at[c], edge_send.at[d, c], hop_recv.at[c],
+            edge_source(d, c), hop.at[c], edge_send.at[d], hop_recv.at[c],
             az=az - way if d == 0 else az + way,
         )
 
@@ -217,11 +217,12 @@
 
     def pack(r, held):
         mine = lane == r
+        before = lane == lax.rem(r + 127, 128)
         got = []
         for f in range(3):
-            left = pltpu.roll(cells[f, r, :, :128], r, 1)
+            left = pltpu.roll(cells[f, r, :, :128], lax.rem(r + 127, 128), 1)
             right = pltpu.roll(cells[f, r, :, 128:], lax.rem(r + 1, 128), 1)
-            got.append(jnp.where(mine, left, held[2 * f]))
+            got.append(jnp.where(before, left, held[2 * f]))
             got.append(jnp.where(mine, right, held[2 * f + 1]))
         return tuple(got)
 
@@ -231,6 +232,19 @@
     for f in range(3):
         packed[0, f] = columns[2 * f]
         packed[1, f] = columns[2 * f + 1]
+
+    to_left = remote(packed.at[0], sides.at[1], side_send.at[0], side_recv.at[1], ax=ax - 1)
+    to_right = remote(packed.at[1], sides.at[0], side_send.at[1], side_recv.at[0], ax=ax + 1)
+
+    @pl.when(has_left)
+    def _():
+        pl.when(even)(lambda: pl.semaphore_wait(ready.at[2], 1))
+        to_left.start()
+
+    @pl.when(has_right)
+    def _():
+        pl.when(even)(lambda: pl.semaphore_wait(ready.at[3], 1))
+        to_right.start()
 
     @pl.when(az < 3)
     def _():
@@ -244,19 +258,6 @@
         pl.semaphore_wait(ready.at[0], 1)
         start(0)
 
-    to_left = remote(packed.at[0], sides.at[1], side_send.at[0], side_recv.at[1], ax=ax - 1)
-    to_right = remote(packed.at[1], sides.at[0], side_send.at[1], side_recv.at[0], ax=ax + 1)
-
-    @pl.when(has_left)
-    def _():
-        pl.when(even)(lambda: pl.semaphore_wait(ready.at[2], 1))
-        to_left.start()
-
-    @pl.when(has_right)
-    def _():
-        pl.when(even)(lambda: pl.semaphore_wait(ready.at[3], 1))
-        to_right.start()
-
     @pl.when(low_end)
     def _():
         pl.semaphore_wait(ready.at[6], 1)
@@ -283,6 +284,12 @@
     @pl.when(jnp.logical_not(has_right))
     def _():
         sides[1] = jnp.zeros((3, 8, 128), jnp.float32)
+
+    in_even = lax.rem(lane, 2) == 0
+    for f in range(3):
+        from_left, from_right = sides[0, f], sides[1, f]
+        packed_in[0, f] = jnp.where(in_even, from_left, from_right)
+        packed_in[1, f] = jnp.where(in_even, from_right, from_left)
 
     def pick(vapor, wick):
         return jnp.where(is_vapor, jnp.float32(vapor), jnp.float32(wick))
@@ -295,24 +302,22 @@
     advect = pick(1.0, 0.5)
     zero = jnp.float32(0.0)
 
-    def cell_row(r):
+    def cell_row(r, parity):
         inner = jnp.maximum(r - 1, 0)
         outer = jnp.minimum(r + 1, radial - 1)
-        to_last = lax.rem(255 - r, 128)
         to_first = lax.rem(128 - r, 128)
         center, laplace, gradient = [], [], []
         for f in range(3):
             c = [cells[f, r, :, :128], cells[f, r, :, 128:]]
             plus = [pltpu.roll(c[0], 127, 1), pltpu.roll(c[1], 127, 1)]
             minus = [pltpu.roll(c[0], 1, 1), pltpu.roll(c[1], 1, 1)]
-            from_right = pltpu.roll(sides[1, f], to_last, 1)
-            from_left = pltpu.roll(sides[0, f], to_first, 1)
+            beside = pltpu.roll(packed_in[parity, f], to_first, 1)
             ax_plus = [
                 jnp.where(last_lane, plus[1], plus[0]),
-                jnp.where(last_lane, from_right, plus[1]),
+                jnp.where(last_lane, beside, plus[1]),
             ]
             ax_minus = [
-                jnp.where(first_lane, from_left, minus[0]),
+                jnp.where(first_lane, beside, minus[0]),
                 jnp.where(first_lane, minus[0], minus[1]),
             ]
             laps, grads = [], []
@@ -350,7 +355,7 @@
     @pl.loop(0, turns)
     def _(i):
         for k in range(unroll):
-            cell_row(i * unroll + k)
+            cell_row(i * unroll + k, k % 2)
 
         pl.when(jnp.logical_and(lifts, i == turns // 4 - 1))(pass_strips)
         pl.when(jnp.logical_and(az == 12, i == turns // 4 - 1))(start_late)
@@ -444,14 +449,12 @@
         )
         out[0, radial - 1, :, lanes] += dt * jnp.where(is_vapor, 0.0, heat)
 
-    @pl.loop(0, chunks)
-    def _(c):
-        edge_copy(0, c).wait_send()
-        edge_copy(1, c).wait_send()
+    for d in range(2):
+        remote(edges.at[d], edges.at[d], edge_send.at[d], edge_recv.at[d, 0], az=nxt).wait_send()
 
     @pl.when(jnp.logical_or(inner, jnp.logical_and(region == 1, at_end)))
     def _():
-        @pl.loop(jnp.where(at_end, 0, 5), jnp.where(at_end, mine, chunks))
+        @pl.loop(jnp.where(at_end, 0, jnp.where(az == 1, round_about[1], round_about[0])), jnp.where(at_end, mine, chunks))
         def _(c):
             onward_copy(0, c).wait_send()
 
@@ -506,13 +509,14 @@
             pltpu.VMEM((2, 8, ax_cells), f32),
             pltpu.VMEM((2, 3, 8, 128), f32),
             pltpu.VMEM((2, 3, 8, 128), f32),
+            pltpu.VMEM((2, 3, 8, 128), f32),
             pltpu.VMEM((16, 8, 256), f32),
             pltpu.VMEM((16, 8, 256), f32),
             pltpu.VMEM((2, 8, 256), f32),
             dma((4,)),
             dma((2,)),
             dma((2,)),
-            dma((2, chunks)),
+            dma((2,)),
             dma((2, chunks)),
             dma((chunks,)),
             dma((chunks,)),

time: 23.7 us -> 23.6 us (level)
  no operation moved by 1% of the time
where the time goes in v7:
time: 23.6 us; the launch traced here: 23.5 us
  Pallas kernels  23.5 us (100%)
    pallas_call x1, Pallas kernels, on_device(): pl.pallas_call(step_kernel, out_shape=pltpu.VMEM(shape, f32), in_specs=[h...  21.8 us
    pallas_call x1, Pallas kernels, on_device(): pl.pallas_call(store_kernel, out_shape=jax.ShapeDtypeStruct(shape, f32),...  1.69 us

profile of v7, /device:TPU:1, one launch (start us, length us, event | category | flops | bytes accessed | tf_op | source)
XLA Modules:
  0.0 23.5 jit_solution(11583646599427571745)
XLA Ops:
  0.0 21.8 %shard_map.46.new = f32[3,128,8,256]{3,2,1,0:T(8,128)S(1)} custom-call(f32[3,128,8,256]{3,2,1,0:T(8,128)} %bitcast.5, f32[128,8,256]{2,1,0:T(8,128)} %bitcast.6, s32[2,128]{1,0:T(2,128)} %bitcast.7, s32[2,128]{1,0:T(2,128)} %bitcast.8), custom_call_target="tpu_custom_call" | custom-call | flops 31457280 | bytes 7340032 | tf_op jit(solution)/shard_map/pallas_call | solution.py:497
  21.8 1.7 %shard_map.47 = f32[3,128,8,256]{3,2,1,0:T(8,128)} custom-call(f32[3,128,8,256]{3,2,1,0:T(8,128)S(1)} %shard_map.46.new), custom_call_target="tpu_custom_call" | custom-call | tf_op jit(solution)/shard_map/pallas_call | solution.py:541

commit v8 on v7

--- a/solution.py
+++ b/solution.py
@@ -14,8 +14,8 @@
 
 def step_kernel(
     state, conduct, zone_ref, place_ref, out,
-    zones, placement, cells, kappa, edges, hop, lift, packed, packed_in, sides, strips, turned, facing,
-    load_sem, lift_send, lift_recv, edge_send, edge_recv, hop_send, hop_recv, side_send, side_recv,
+    zones, placement, cells, kappa, edges, hop, packed, packed_in, sides, strips, turned, facing,
+    load_sem, edge_send, edge_recv, hop_send, hop_recv, side_send, side_recv,
     strip_send, strip_recv, turn_send, turn_recv, ready,
 ):
     region = lax.axis_index("region")
@@ -115,28 +115,11 @@
         remote(strip_source(q), strips.at[az], strip_send, strip_recv, az=1 + q)
         for q in range(2)
     ]
-    lifted = az < 0
-    lifts = az < 0
-    lift_copies = [
-        remote(strip_source(q), lift.at[q], lift_send.at[q], lift_recv.at[q], az=12)
-        for q in range(2)
-    ]
-    lifted_copies = [
-        remote(lift.at[q], strips.at[15], lift_send.at[q], strip_recv, az=1 + q)
-        for q in range(2)
-    ]
-
     def start_all(copies):
         for c in copies:
             c.start()
 
-    def pass_strips():
-        for q in range(2):
-            lift_copies[q].wait_recv()
-            lifted_copies[q].start()
-
-    pl.when(jnp.logical_and(az > 2, jnp.logical_not(lifted)))(lambda: start_all(strip_copies))
-    pl.when(lifted)(lambda: start_all(lift_copies))
+    pl.when(az > 2)(lambda: start_all(strip_copies))
 
     far = (high_end, low_end)
     neighbour = (nxt, prv)
@@ -151,7 +134,7 @@
         )
 
     round_about = (
-        jnp.where(az < 8, 7, 5),
+        jnp.where(az < 8, jnp.where(odd, 5, 8), 5),
         jnp.where(az < 4, 7, jnp.where(az < 12, 5, 6)),
     )
     rest_inner = (jnp.logical_and(high_end, az > 8), jnp.logical_and(low_end, az == 0))
@@ -357,7 +340,6 @@
         for k in range(unroll):
             cell_row(i * unroll + k, k % 2)
 
-        pl.when(jnp.logical_and(lifts, i == turns // 4 - 1))(pass_strips)
         pl.when(jnp.logical_and(az == 12, i == turns // 4 - 1))(start_late)
         pl.when(jnp.logical_and(az == 0, i == 3 * turns // 4 - 1))(start_late)
         quarter = lax.div(i + 1, turns // 4)
@@ -465,15 +447,10 @@
         strip_copies[0].wait_send()
         remote(turned, turned, turn_send, turn_recv.at[0], az=az).wait_send()
 
-    @pl.when(jnp.logical_not(jnp.logical_or(is_worker, lifted)))
+    @pl.when(jnp.logical_not(is_worker))
     def _():
         two = facing
         remote(two, two, strip_send, strip_recv, az=az).wait_send()
-
-    @pl.when(jnp.logical_or(lifted, lifts))
-    def _():
-        for c in lift_copies:
-            c.wait_send()
 
 
 def store_kernel(new, out, sems):
@@ -506,7 +483,6 @@
             pltpu.VMEM(shape[1:], f32),
             pltpu.VMEM((2, 3, radial, 1, ax_cells), f32),
             pltpu.VMEM((chunks, 3, radial // chunks, 1, ax_cells), f32),
-            pltpu.VMEM((2, 8, ax_cells), f32),
             pltpu.VMEM((2, 3, 8, 128), f32),
             pltpu.VMEM((2, 3, 8, 128), f32),
             pltpu.VMEM((2, 3, 8, 128), f32),
@@ -514,8 +490,6 @@
             pltpu.VMEM((16, 8, 256), f32),
             pltpu.VMEM((2, 8, 256), f32),
             dma((4,)),
-            dma((2,)),
-            dma((2,)),
             dma((2,)),
             dma((2, chunks)),
             dma((chunks,)),

time: 23.6 us -> 23.5 us (level)
  no operation moved by 1% of the time
where the time goes in v8:
time: 23.5 us; the launch traced here: 23.4 us
  Pallas kernels  23.4 us (100%)
    pallas_call x1, Pallas kernels, on_device(): pl.pallas_call(step_kernel, out_shape=pltpu.VMEM(shape, f32), in_specs=[h...  21.7 us
    pallas_call x1, Pallas kernels, on_device(): pl.pallas_call(store_kernel, out_shape=jax.ShapeDtypeStruct(shape, f32),...  1.69 us

profile of v8, /device:TPU:1, one launch (start us, length us, event | category | flops | bytes accessed | tf_op | source)
XLA Modules:
  0.0 23.4 jit_solution(10193595608291230075)
XLA Ops:
  0.0 21.7 %shard_map.46.new = f32[3,128,8,256]{3,2,1,0:T(8,128)S(1)} custom-call(f32[3,128,8,256]{3,2,1,0:T(8,128)} %bitcast.5, f32[128,8,256]{2,1,0:T(8,128)} %bitcast.6, s32[2,128]{1,0:T(2,128)} %bitcast.7, s32[2,128]{1,0:T(2,128)} %bitcast.8), custom_call_target="tpu_custom_call" | custom-call | flops 31457280 | bytes 7340032 | tf_op jit(solution)/shard_map/pallas_call | solution.py:474
  21.8 1.7 %shard_map.47 = f32[3,128,8,256]{3,2,1,0:T(8,128)} custom-call(f32[3,128,8,256]{3,2,1,0:T(8,128)S(1)} %shard_map.46.new), custom_call_target="tpu_custom_call" | custom-call | tf_op jit(solution)/shard_map/pallas_call | solution.py:515

commit v9 on v8

--- a/solution.py
+++ b/solution.py
@@ -63,7 +63,7 @@
     pl.when(low_end)(lambda: signal(barrier, az=az + 3))
     pl.when(jnp.logical_and(inner, az > 8))(lambda: signal(barrier, az=az + 2))
     pl.when(even)(lambda: signal(barrier, ax=ax + 1))
-    pl.when(jnp.logical_and(even, has_left))(lambda: signal(barrier, ax=ax - 1))
+    pl.when(jnp.logical_and(odd, has_right))(lambda: signal(barrier, ax=ax + 1))
 
     loads = [
         pltpu.make_async_copy(src, dst, load_sem.at[i])
@@ -92,7 +92,7 @@
         + prev_first.astype(jnp.int32)
         + high_end.astype(jnp.int32)
         + jnp.logical_and(high_end, az > 8).astype(jnp.int32)
-        + jnp.where(odd, 1 + has_right.astype(jnp.int32), 0)
+        + has_left.astype(jnp.int32)
         + jnp.minimum(az, 2)
         + jnp.logical_and(is_worker, region == 1).astype(jnp.int32)
     )
@@ -181,10 +181,7 @@
         lambda: start_part(1, jnp.where(low_end, round_about[1], 0), chunks)
     )
 
-    @pl.when(odd)
-    def _():
-        signal(ready.at[3], ax=ax - 1)
-        pl.when(has_right)(lambda: signal(ready.at[2], ax=ax + 1))
+    pl.when(has_left)(lambda: signal(ready.at[3], ax=ax - 1))
 
     for c in loads:
         c.wait()
@@ -221,12 +218,11 @@
 
     @pl.when(has_left)
     def _():
-        pl.when(even)(lambda: pl.semaphore_wait(ready.at[2], 1))
         to_left.start()
 
     @pl.when(has_right)
     def _():
-        pl.when(even)(lambda: pl.semaphore_wait(ready.at[3], 1))
+        pl.semaphore_wait(ready.at[3], 1)
         to_right.start()
 
     @pl.when(az < 3)

time: 23.5 us -> 23.2 us (0.987)
  Pallas kernels: 23.4 us -> 23.1 us
    pallas_call x1, Pallas kernels: 21.7 us -> 21.4 us  [on_device(): pl.pallas_call(step_kernel, out_shape=pltpu.VMEM(shape, f32), in_specs=[h...]
where the time goes in v9:
time: 23.2 us; the launch traced here: 23.1 us
  Pallas kernels  23.1 us (100%)
    pallas_call x1, Pallas kernels, on_device(): pl.pallas_call(step_kernel, out_shape=pltpu.VMEM(shape, f32), in_specs=[h...  21.4 us
    pallas_call x1, Pallas kernels, on_device(): pl.pallas_call(store_kernel, out_shape=jax.ShapeDtypeStruct(shape, f32),...  1.69 us

profile of v9, /device:TPU:1, one launch (start us, length us, event | category | flops | bytes accessed | tf_op | source)
XLA Modules:
  0.0 23.1 jit_solution(14011374984344917596)
XLA Ops:
  0.0 21.4 %shard_map.46.new = f32[3,128,8,256]{3,2,1,0:T(8,128)S(1)} custom-call(f32[3,128,8,256]{3,2,1,0:T(8,128)} %bitcast.5, f32[128,8,256]{2,1,0:T(8,128)} %bitcast.6, s32[2,128]{1,0:T(2,128)} %bitcast.7, s32[2,128]{1,0:T(2,128)} %bitcast.8), custom_call_target="tpu_custom_call" | custom-call | flops 31457280 | bytes 7340032 | tf_op jit(solution)/shard_map/pallas_call | solution.py:470
  21.4 1.7 %shard_map.47 = f32[3,128,8,256]{3,2,1,0:T(8,128)} custom-call(f32[3,128,8,256]{3,2,1,0:T(8,128)S(1)} %shard_map.46.new), custom_call_target="tpu_custom_call" | custom-call | tf_op jit(solution)/shard_map/pallas_call | solution.py:511

commit v10 on v9

--- a/solution.py
+++ b/solution.py
@@ -134,7 +134,7 @@
         )
 
     round_about = (
-        jnp.where(az < 8, jnp.where(odd, 5, 8), 5),
+        jnp.where(az < 8, jnp.where(odd, 3, 8), 5),
         jnp.where(az < 4, 7, jnp.where(az < 12, 5, 6)),
     )
     rest_inner = (jnp.logical_and(high_end, az > 8), jnp.logical_and(low_end, az == 0))

time: 23.2 us -> 23.2 us (level)
  no operation moved by 1% of the time
where the time goes in v10:
time: 23.2 us; the launch traced here: 23.1 us
  Pallas kernels  23.1 us (100%)
    pallas_call x1, Pallas kernels, on_device(): pl.pallas_call(step_kernel, out_shape=pltpu.VMEM(shape, f32), in_specs=[h...  21.4 us
    pallas_call x1, Pallas kernels, on_device(): pl.pallas_call(store_kernel, out_shape=jax.ShapeDtypeStruct(shape, f32),...  1.69 us

profile of v10, /device:TPU:1, one launch (start us, length us, event | category | flops | bytes accessed | tf_op | source)
XLA Modules:
  0.0 23.1 jit_solution(8581095539637290507)
XLA Ops:
  0.0 21.4 %shard_map.46.new = f32[3,128,8,256]{3,2,1,0:T(8,128)S(1)} custom-call(f32[3,128,8,256]{3,2,1,0:T(8,128)} %bitcast.5, f32[128,8,256]{2,1,0:T(8,128)} %bitcast.6, s32[2,128]{1,0:T(2,128)} %bitcast.7, s32[2,128]{1,0:T(2,128)} %bitcast.8), custom_call_target="tpu_custom_call" | custom-call | flops 31457280 | bytes 7340032 | tf_op jit(solution)/shard_map/pallas_call | solution.py:470
  21.4 1.7 %shard_map.47 = f32[3,128,8,256]{3,2,1,0:T(8,128)} custom-call(f32[3,128,8,256]{3,2,1,0:T(8,128)S(1)} %shard_map.46.new), custom_call_target="tpu_custom_call" | custom-call | tf_op jit(solution)/shard_map/pallas_call | solution.py:511
